TPU v7x, 128 devices: a whole 4x4x4 slice. The times are simulated.
128 devices in a mesh: snap: 8 (over z_lo, y), height: 16 (over z_hi, x, core).
Axes of the slice: x: 4, y: 4, z: 4 (z_hi: 2, z_lo: 2; z = z_hi * 2 + z_lo), core: 2. Of those that a mesh axis runs over, the one named last changes fastest.
Arguments:
- resolved: bfloat16 [128, 3, 128, 16, 2, 128], P('snap', None, 'height'), may hold values from -6 to 6
- drain: bfloat16 [128, 3, 128, 16, 2, 128], P('snap', None, 'height'), may hold values from -6 to 6
- pair_list: int32 [256, 2], replicated, may hold values from 0 to 127, as said below
- ridge_index: int32 [256], replicated, may hold values from 0 to 3
Outputs:
- predicted: float32 [128, 3, 128, 2, 256], P('snap', None, 'height')
- misfit: float32 [1], replicated
Inputs may be any that keep to these rules, and one draw needn't show every extreme that they name: `pair_list`: each row names a streamwise mode below 16 and a spanwise wavenumber below 128; no row repeats.
All inputs are finite; a program needn't handle non-finite values.
Results may differ from a plain program's by a relative error of at most 0.0032.
Values sent between devices are 32-bit elements; how exact they have to be, the bound alone decides.
No kernel may reach another device: no remote copies, remote signals or barrier semaphores. Data moves between devices by JAX's collectives and lax.ppermute only.
A program may use at most 128 MiB of HBM per device.

v0:
```python
import math

import jax
import jax.numpy as jnp
from jax import lax
from jax.sharding import PartitionSpec as P


def twiddles(length):
    grid = jnp.arange(length, dtype=jnp.int32)
    phase = grid[:, None] * grid[None, :] % length
    theta = phase.astype(jnp.float32) * (2.0 * math.pi / length)
    scaling = 1.0 / math.sqrt(length)
    cosine = jnp.cos(theta) * scaling
    sine = jnp.sin(theta) * scaling
    upper = jnp.concatenate([cosine, -sine], axis=1)
    lower = jnp.concatenate([sine, cosine], axis=1)
    return jnp.concatenate([upper, lower], axis=0).astype(jnp.bfloat16)


def per_device(resolved, drain, pair_list, ridge_index):
    snap_local, components, height_local, mode_count, halves, points = resolved.shape
    snap_count = lax.axis_size("snap")
    height_count = lax.axis_size("height")
    owners = snap_count * height_count
    pair_total = pair_list.shape[0]
    pair_local = pair_total // owners
    twiddle = twiddles(points)
    row_count = snap_local * components * height_local
    highest = lax.Precision.HIGHEST

    def spectrum(values):
        product = jnp.dot(
            values.reshape(-1, 2 * points), twiddle, preferred_element_type=jnp.float32
        )
        product = product.reshape(row_count, mode_count, 2, points)
        picked = product[:, pair_list[:, 0], :, pair_list[:, 1]]
        return jnp.transpose(picked, (1, 2, 0)).reshape(
            snap_local, components, height_local, 2, pair_total
        )

    spec_x = spectrum(resolved)
    spec_y = spectrum(drain)
    arrivals = (
        lax.all_to_all(spec_x[None], ("snap", "height"), split_axis=5, concat_axis=0, tiled=True),
        lax.all_to_all(spec_y[None], ("snap", "height"), split_axis=5, concat_axis=0, tiled=True),
    )

    def settle(arrived):
        arrived = arrived.reshape(
            snap_count, height_count, snap_local, components, height_local, 2, pair_local
        )
        arrived = jnp.transpose(arrived, (6, 5, 0, 2, 3, 1, 4))
        return arrived.reshape(
            pair_local, 2, snap_count * snap_local, components * height_count * height_local
        )

    owned_x = settle(arrivals[0])
    owned_y = settle(arrivals[1])
    total_snaps = owned_x.shape[2]
    real_x = owned_x[:, 0]
    imag_x = owned_x[:, 1]
    stacked_x = jnp.concatenate(
        [jnp.concatenate([real_x, imag_x], 2), jnp.concatenate([-imag_x, real_x], 2)], 1
    )
    stacked_y = owned_y.reshape(pair_local, 2 * total_snaps, -1)
    feature_count = stacked_y.shape[2]
    owner_index = lax.axis_index("snap") * height_count + lax.axis_index("height")
    levels = lax.dynamic_slice_in_dim(ridge_index, owner_index * pair_local, pair_local, 0)
    ridge = 0.25 * jnp.exp2(levels.astype(jnp.float32))
    gram = jnp.einsum("psf,psg->pfg", stacked_x, stacked_x, precision=highest) / total_snaps
    gram = gram + ridge[:, None, None] * jnp.eye(2 * feature_count, dtype=jnp.float32)
    moments = jnp.einsum("psf,psg->pfg", stacked_x, stacked_y, precision=highest) / total_snaps
    factor = jnp.linalg.cholesky(gram)
    halfway = lax.linalg.triangular_solve(
        factor, moments, left_side=True, lower=True, transpose_a=False
    )
    weights = lax.linalg.triangular_solve(
        factor, halfway, left_side=True, lower=True, transpose_a=True
    )
    fitted = jnp.einsum("psf,pfg->psg", stacked_x, weights, precision=highest)
    totals = lax.psum(
        (jnp.sum((stacked_y - fitted) ** 2), jnp.sum(stacked_y**2)), ("snap", "height")
    )
    misfit = (totals[0] / totals[1]).reshape(1)
    fitted = fitted.reshape(
        pair_local, 2, snap_count, snap_local, components, height_count, height_local
    )
    outgoing = jnp.transpose(fitted, (2, 5, 3, 4, 6, 1, 0)).reshape(
        owners, snap_local, components, height_local, 2, pair_local
    )
    returned = lax.all_to_all(outgoing, ("snap", "height"), split_axis=0, concat_axis=5, tiled=True)
    predicted = returned.reshape(snap_local, components, height_local, 2, pair_total)
    return (predicted, misfit)


def solution(mesh):
    return jax.shard_map(
        per_device,
        mesh=mesh,
        in_specs=(
            P("snap", None, "height", None, None, None),
            P("snap", None, "height", None, None, None),
            P(),
            P(),
        ),
        out_specs=(P("snap", None, "height", None, None), P()),
        check_vma=False,
    )
```

profile of v0, /device:TPU:1, one launch (start us, length us, event | category | flops | bytes accessed | tf_op | source)
XLA Modules:
  0.0 782.7 jit_solution(8975611457506598319)
XLA Ops:
  1.2 5.6 convolution_bitcast_fusion.1
  6.8 6.6 copy.203
  13.4 8.2 %reshape.140 = f32[384,16,2,128]{3,2,1,0:T(2,128)} reshape(f32[6144,256]{1,0:T(8,128)} %copy.203) | data formatting | bytes 12582912 | tf_op jit(solution)/shard_map/reshape | solution.py:36
  21.6 12.0 %copy.204 = f32[384,16,2,128]{0,2,3,1:T(2,128)} copy(f32[384,16,2,128]{3,2,1,0:T(2,128)} %reshape.140) | data formatting | bytes 12582912 | tf_op jit(solution)/shard_map/reshape | solution.py:36
  33.7 4.7 gather_fusion
  38.8 5.1 copy.206
  44.0 5.5 reshape.185
  49.5 11.8 %all-to-all-start = ((f32[128,1,1536]{2,1,0:T(1,128)}), f32[128,1,1536]{2,1,0:T(1,128)S(1)}, u32[]{:S(2)}, u32[]{:S(2)}) async-start(f32[128,1,1536]{2,1,0:T(1,128)} %reshape.185), calls=%async_computation | async-start | bytes 1572864 | tf_op jit(solution)/shard_map/all_to_all | solution.py:45
  61.3 5.6 convolution_bitcast_fusion
  66.9 6.6 copy.225
  73.5 8.2 %reshape.144 = f32[384,16,2,128]{3,2,1,0:T(2,128)} reshape(f32[6144,256]{1,0:T(8,128)} %copy.225) | data formatting | bytes 12582912 | tf_op jit(solution)/shard_map/reshape | solution.py:36
  81.8 12.0 %copy.226 = f32[384,16,2,128]{0,2,3,1:T(2,128)} copy(f32[384,16,2,128]{3,2,1,0:T(2,128)} %reshape.144) | data formatting | bytes 12582912 | tf_op jit(solution)/shard_map/reshape | solution.py:36
  93.8 4.7 gather_fusion.1
  98.9 5.1 copy.228
  104.1 5.5 reshape.183
  111.7 10.7 %all-to-all-start.1 = ((f32[128,1,1536]{2,1,0:T(1,128)}), f32[128,1,1536]{2,1,0:T(1,128)}, u32[]{:S(2)}, u32[]{:S(2)}) async-start(f32[128,1,1536]{2,1,0:T(1,128)} %reshape.183), calls=%async_computation.1 | async-start | bytes 1572864 | tf_op jit(solution)/shard_map/all_to_all | solution.py:46
  132.8 9.1 %copy.209 = f32[2,2,8,16,3,16,8]{3,2,6,5,4,1,0:T(8,128)} copy(f32[2,2,8,16,3,16,8]{3,6,1,4,0,5,2:T(8,128)} %bitcast.183) | data formatting | bytes 1572864 | tf_op jit(solution)/shard_map/transpose | solution.py:53
  141.8 4.3 reshape.142
  154.6 15.0 %reshape.184 = f32[256,1,3,2,8,16]{5,4,3,2,1,0:T(8,128)} reshape(f32[128,1536]{1,0:T(8,128)S(1)} %reduce.37) | data formatting | bytes 1572864
  169.6 9.1 %copy.231 = f32[2,2,8,16,3,16,8]{3,2,1,6,5,4,0:T(8,128)} copy(f32[2,2,8,16,3,16,8]{3,6,1,4,0,5,2:T(8,128)} %bitcast.179) | data formatting | bytes 1572864 | tf_op jit(solution)/shard_map/transpose | solution.py:53
  178.7 4.9 reshape_reshape.3
  183.6 8.2 %fusion.49 = f32[2,768,768]{2,1,0:T(8,128)} fusion(f32[2,128,384]{2,1,0:T(8,128)} %bitcast.190, f32[2,128,384]{2,1,0:T(8,128)} %bitcast_negate_fusion, f32[2,128,384]{2,1,0:T(8,128)S(1)} %bitcast.187), kind=kOutput, calls=%fused_computation.79 | convolution fusion | flops 3625058304 | bytes 5898240 | tf_op jit(solution)/shard_map/psf,psg->pfg/dot_general | solution.py:71
  191.8 6.5 convolution_multiply_fusion
  199.4 4.7 multiply_bitcast_fusion
  204.2 6.1 copy.213
  210.2 5.6 add_multiply_fusion
  218.1 23.9 %custom-call.54 = f32[2,128,128]{2,1,0:T(8,128)S(1)} custom-call(f32[2,128,128]{2,1,0:T(8,128)S(1)} %cholesky.426), custom_call_target="Cholesky" | custom-call | tf_op jit(solution)/shard_map/jit(cholesky)/cholesky | solution.py:74
  241.9 19.7 %custom-call.55 = f32[2,1,128,128]{2,3,1,0:T(8,128)S(1)} custom-call(f32[2,1,128,128]{3,2,1,0:T(8,128)S(1)} %select_bitcast_fusion.4), custom_call_target="InvertDiagBlocksLowerTriangular" | custom-call | tf_op jit(solution)/shard_map/jit(cholesky)/cholesky | solution.py:74
  268.7 23.5 %custom-call.56 = f32[2,128,128]{2,1,0:T(8,128)S(1)} custom-call(f32[2,128,128]{2,1,0:T(8,128)S(1)} %cholesky.430), custom_call_target="Cholesky" | custom-call | tf_op jit(solution)/shard_map/jit(cholesky)/cholesky | solution.py:74
  292.9 19.8 %custom-call.57 = f32[2,1,128,128]{2,3,1,0:T(8,128)S(1)} custom-call(f32[2,1,128,128]{3,2,1,0:T(8,128)S(1)} %get-tuple-element.47), custom_call_target="InvertDiagBlocksLowerTriangular" | custom-call | tf_op jit(solution)/shard_map/jit(cholesky)/cholesky | solution.py:74
  316.7 23.5 %custom-call.58 = f32[2,128,128]{2,1,0:T(8,128)S(1)} custom-call(f32[2,128,128]{2,1,0:T(8,128)S(1)} %cholesky.435), custom_call_target="Cholesky" | custom-call | tf_op jit(solution)/shard_map/jit(cholesky)/cholesky | solution.py:74
  340.8 19.7 %custom-call.59 = f32[2,1,128,128]{2,3,1,0:T(8,128)S(1)} custom-call(f32[2,1,128,128]{3,2,1,0:T(8,128)S(1)} %get-tuple-element.45), custom_call_target="InvertDiagBlocksLowerTriangular" | custom-call | tf_op jit(solution)/shard_map/jit(cholesky)/cholesky | solution.py:74
  364.5 23.7 %custom-call.60 = f32[2,128,128]{2,1,0:T(8,128)S(1)} custom-call(f32[2,128,128]{2,1,0:T(8,128)S(1)} %cholesky.440), custom_call_target="Cholesky" | custom-call | tf_op jit(solution)/shard_map/jit(cholesky)/cholesky | solution.py:74
  388.8 19.7 %custom-call.61 = f32[2,1,128,128]{2,3,1,0:T(8,128)S(1)} custom-call(f32[2,1,128,128]{3,2,1,0:T(8,128)S(1)} %get-tuple-element.43), custom_call_target="InvertDiagBlocksLowerTriangular" | custom-call | tf_op jit(solution)/shard_map/jit(cholesky)/cholesky | solution.py:74
  412.3 23.5 %custom-call.62 = f32[2,128,128]{2,1,0:T(8,128)S(1)} custom-call(f32[2,128,128]{2,1,0:T(8,128)S(1)} %cholesky.445), custom_call_target="Cholesky" | custom-call | tf_op jit(solution)/shard_map/jit(cholesky)/cholesky | solution.py:74
  436.4 20.1 %custom-call.63 = f32[2,1,128,128]{2,3,1,0:T(8,128)S(1)} custom-call(f32[2,1,128,128]{3,2,1,0:T(8,128)S(1)} %get-tuple-element.41), custom_call_target="InvertDiagBlocksLowerTriangular" | custom-call | tf_op jit(solution)/shard_map/jit(cholesky)/cholesky | solution.py:74
  459.7 23.5 %custom-call.64 = f32[2,128,128]{2,1,0:T(8,128)S(1)} custom-call(f32[2,128,128]{2,1,0:T(8,128)S(1)} %convolution_subtract_fusion.12), custom_call_target="Cholesky" | custom-call | tf_op jit(solution)/shard_map/jit(cholesky)/cholesky | solution.py:74
  484.7 5.4 select_select_fusion
  490.1 21.1 %while.1 = (s32[]{:T(128)}, f32[2,768,768]{2,1,0:T(8,128)}, s32[6,2]{0,1:T(2,128)S(1)}, f32[6,2,128,128]{3,2,0,1:T(8,128)}, s32[]{:T(128)}) while((s32[]{:T(128)}, f32[2,768,768]{2,1,0:T(8,128)}, s32[6,2]{0,1:T(2,128)S(1)}, f32[6,2,128,128]{3,2,0,1:T(8,128)}, s32[]{:T(128)}) %tuple.49), condition=%wide.while_cond, body=%wide.while_body.sunk | while | flops 2 | bytes 263777 | solution.py:78
  511.2 118.9 %custom-call.65 = f32[2,6,128,128]{2,3,1,0:T(8,128)S(1)} custom-call(f32[2,6,128,128]{3,2,1,0:T(8,128)} %bitcast.197), custom_call_target="InvertDiagBlocksLowerTriangular" | custom-call | tf_op jit(solution)/shard_map/triangular_solve | solution.py:78
  653.6 4.0 reshape.146
  657.6 7.4 copy.274
  665.0 5.5 reshape.187
  670.5 10.1 %all-to-all-start.2 = ((f32[128,1,1536]{2,1,0:T(1,128)}), f32[128,1,1536]{2,1,0:T(1,128)S(1)}, u32[]{:S(2)}, u32[]{:S(2)}) async-start(f32[128,1,1536]{2,1,0:T(1,128)} %reshape.187), calls=%async_computation.2 | async-start | bytes 1572864 | tf_op jit(solution)/shard_map/all_to_all | solution.py:92
  680.6 8.3 %copy.272 = f32[8,16,16,3,8,2,2]{1,0,4,6,5,3,2:T(8,128)} copy(f32[8,16,16,3,8,2,2]{2,4,5,3,6,1,0:T(8,128)} %bitcast.180) | data formatting | bytes 1572864 | tf_op jit(solution)/shard_map/reshape | solution.py:50
  688.9 5.1 fusion
  694.0 67.2 %all-reduce.1 = (f32[]{:T(128)}, f32[]{:T(128)}) all-reduce(f32[]{:T(128)} %get-tuple-element.63, f32[]{:T(128)} %fusion), channel_id=1, replica_groups=mesh['snap'=8,'height'=16] {'snap','height'}, use_global_device_ids=true, to_apply=%region_13.14 | all-reduce | flops 2 | bytes 16 | tf_op jit(solution)/shard_map/psum | solution.py:82
  775.8 5.4 copy.250
  (139 shorter events, 109.6 us)
Async XLA Ops:
  21.6 12.0 %copy-start.11 = (s32[256,2]{0,1:T(2,128)S(1)}, s32[256,2]{0,1:T(2,128)}, u32[]{:S(2)}) copy-start(s32[256,2]{0,1:T(2,128)} %param.6) | copy-start | bytes 6148
  49.5 62.2 %all-to-all-start = ((f32[128,1,1536]{2,1,0:T(1,128)}), f32[128,1,1536]{2,1,0:T(1,128)S(1)}, u32[]{:S(2)}, u32[]{:S(2)}) async-start(f32[128,1,1536]{2,1,0:T(1,128)} %reshape.185), calls=%async_computation | async-start | bytes 1572864 | tf_op jit(solution)/shard_map/all_to_all | solution.py:45
  104.1 18.3 %copy-start.13 = (s32[256]{0:T(256)S(1)}, s32[256]{0:T(256)}, u32[]{:S(2)}) copy-start(s32[256]{0:T(256)} %param.7) | copy-start | bytes 3076
  111.7 11.3 %copy-start.7 = (f32[128,1,1536]{2,1,0:T(1,128)}, f32[128,1,1536]{2,1,0:T(1,128)S(1)}, u32[]{:S(2)}) copy-start(f32[128,1,1536]{2,1,0:T(1,128)S(1)} %all-to-all-done) | copy-start | bytes 2359300
  111.7 39.3 %all-to-all-start.1 = ((f32[128,1,1536]{2,1,0:T(1,128)}), f32[128,1,1536]{2,1,0:T(1,128)}, u32[]{:S(2)}, u32[]{:S(2)}) async-start(f32[128,1,1536]{2,1,0:T(1,128)} %reshape.183), calls=%async_computation.1 | async-start | bytes 1572864 | tf_op jit(solution)/shard_map/all_to_all | solution.py:46
  183.6 8.2 %copy-start.3 = (f32[2,1,128,384]{3,2,0,1:T(8,128)S(1)}, f32[2,1,128,384]{3,2,0,1:T(8,128)}, u32[]{:S(2)}) copy-start(f32[2,1,128,384]{3,2,0,1:T(8,128)} %copy.281) | copy-start | bytes 1179652
  183.6 8.2 %copy-start.5 = (f32[2,128,384]{2,1,0:T(8,128)S(1)}, f32[2,128,384]{2,1,0:T(8,128)}, u32[]{:S(2)}) copy-start(f32[2,128,384]{2,1,0:T(8,128)} %bitcast_negate_fusion) | copy-start | bytes 1179652
  204.2 6.1 copy-start.12
  215.8 2.2 copy-start.1
  364.4 118.8 %copy-start.10 = (pred[128,128]{1,0:T(8,128)(4,1)S(1)}, pred[128,128]{1,0:T(8,128)(4,1)}, u32[]{:S(2)}) copy-start(pred[128,128]{1,0:T(8,128)(4,1)} %iota_compare_fusion.4) | copy-start | bytes 49156
  364.4 120.3 %copy-start.9 = (pred[768,768]{1,0:T(8,128)(4,1)S(1)}, pred[768,768]{1,0:T(8,128)(4,1)}, u32[]{:S(2)}) copy-start(pred[768,768]{1,0:T(8,128)(4,1)} %iota_compare_fusion.2) | copy-start | bytes 1769476
  484.7 5.4 copy-start.14
  484.7 145.4 %copy-start.2 = (f32[2,768,384]{2,1,0:T(8,128)S(1)}, f32[2,768,384]{2,1,0:T(8,128)}, u32[]{:S(2)}) copy-start(f32[2,768,384]{2,1,0:T(8,128)} %convolution_multiply_fusion) | copy-start | bytes 7077892
  630.6 4.3 copy-start
  648.6 1.0 copy-start.4
  648.6 1.1 copy-start.6
  648.6 1.4 copy-start.8
  670.5 92.1 %all-to-all-start.2 = ((f32[128,1,1536]{2,1,0:T(1,128)}), f32[128,1,1536]{2,1,0:T(1,128)S(1)}, u32[]{:S(2)}, u32[]{:S(2)}) async-start(f32[128,1,1536]{2,1,0:T(1,128)} %reshape.187), calls=%async_computation.2 | async-start | bytes 1572864 | tf_op jit(solution)/shard_map/all_to_all | solution.py:92
where the time goes:
time: 791 us; the launch traced here: 783 us
  other arithmetic  400 us (51%)
  local copies, waits for them, and re-layouts  211 us (27%)
  matrix products  67.3 us (9%)
  blocking collectives  67.2 us (8%)
  starting transfers between devices  32.6 us (4%)
    another operation x26, other arithmetic, per_device(): factor = jnp.linalg.cholesky(gram)  245 us
    another operation x4, other arithmetic, per_device(): lax.linalg.triangular_solve(factor, halfway, left_side=True, lower=True,...  126 us
    psum x1, blocking collectives, per_device(): lax.psum((jnp.sum((stacked_y - fitted) ** 2), jnp.sum(stacked_y ** 2)), (...  67.2 us
    unnamed x46, local copies, waits for them, and re-layouts  50.8 us
    reshape x4, local copies, waits for them, and re-layouts, spectrum(): product = product.reshape(row_count, mode_count, 2, points)  40.6 us
    another operation x18, local copies, waits for them, and re-layouts  21 us
    another operation x10, matrix products, per_device(): factor = jnp.linalg.cholesky(gram)  19.4 us
    transpose x2, local copies, waits for them, and re-layouts, settle(): arrived = jnp.transpose(arrived, (6, 5, 0, 2, 3, 1, 4))  18.2 us
  transfers between devices with their start and end apart: 3, of which 0 were waited for; matrix products, arithmetic and copies ran while one was open for 12% of the time, Pallas kernels for 0%

commit v1 on v0

v1 whole, which is shorter than its diff:
```python
import math

import jax
import jax.numpy as jnp
import numpy as np
from jax import lax
from jax.experimental import pallas as pl
from jax.experimental.pallas import tpu as pltpu
from jax.sharding import PartitionSpec as P

HIGHEST = lax.Precision.HIGHEST
BLOCK = 32
LANES = 128


def twiddle_rows(length):
    grid = np.arange(length)
    theta = ((grid[:, None] * grid[None, :]) % length) * (2.0 * math.pi / length)
    scaling = 1.0 / math.sqrt(length)
    cosine = np.cos(theta) * scaling
    sine = np.sin(theta) * scaling
    upper = np.concatenate([cosine, -sine], axis=1)
    lower = np.concatenate([sine, cosine], axis=1)
    table = np.concatenate([upper, lower], axis=0)
    return jnp.asarray(np.ascontiguousarray(table.T), dtype=jnp.bfloat16)


def lane_iota(shape):
    return lax.broadcasted_iota(jnp.int32, shape, len(shape) - 1)


def exact_dot(a, b):
    return lax.dot_general(
        a, b, (((1,), (0,)), ((), ())), precision=HIGHEST, preferred_element_type=jnp.float32
    )


def turn(values, amount):
    amount %= LANES
    return pltpu.roll(values, amount, 1) if amount else values


def swap_blocks(values):
    values = list(values)
    lane = lane_iota(values[0].shape)
    for bit in (1, 2, 4):
        odd = (lane & bit) != 0
        for index in range(8):
            if index & bit:
                continue
            low, high = values[index], values[index | bit]
            values[index] = jnp.where(odd, turn(high, bit), low)
            values[index | bit] = jnp.where(odd, high, turn(low, -bit))
    return values


def spectrum_kernel(pairs_ref, table_ref, x_ref, y_ref, out_ref, masked, wide, packed):
    component = pl.program_id(0)

    @pl.when(component == 0)
    def _():
        for j in range(2):
            lanes = pl.ds(j * LANES, LANES)
            mode = pairs_ref[0:1, lanes].astype(jnp.float32)
            wave = pairs_ref[1:2, lanes].astype(jnp.float32)
            mode = jnp.transpose(jnp.broadcast_to(mode, (LANES, LANES)))
            wave = jnp.transpose(jnp.broadcast_to(wave, (LANES, LANES)))
            chosen = wave == lane_iota((LANES, LANES)).astype(jnp.float32)
            chosen = jnp.where(chosen, 1.0, 0.0).astype(jnp.bfloat16)
            mode = jnp.concatenate([mode, mode], axis=1)
            for r in range(2):
                rows = jnp.dot(
                    chosen, table_ref[r * LANES : (r + 1) * LANES, :], preferred_element_type=jnp.float32
                )
                for m in range(16):
                    masked[pl.ds((j * 2 + r) * LANES, LANES), pl.ds(m * 256, 256)] = jnp.where(
                        mode == float(m), rows, 0.0
                    ).astype(jnp.bfloat16)

    for a, ref in enumerate((x_ref, y_ref)):
        wide[...] = ref[...].reshape(4096, LANES).astype(jnp.float32)
        for part in range(32):
            packed[pl.ds(a * LANES, LANES), pl.ds(part * LANES, LANES)] = wide[
                pl.ds(part, LANES, stride=32), :
            ].astype(jnp.bfloat16)
    product = lax.dot_general(
        masked[...], packed[...], (((1,), (1,)), ((), ())), preferred_element_type=jnp.float32
    )
    for a in range(2):
        for q in range(4):
            for group in range(16):
                row = q * LANES + group * 8
                out_ref[pl.ds(group * 8 * 24 + a * 12 + component * 4 + q, 8, stride=24), :] = product[
                    row : row + 8, a * LANES : (a + 1) * LANES
                ]


def invert_block(block):
    shape = block.shape
    lane = lane_iota(shape)
    sub = lax.broadcasted_iota(jnp.int32, shape, 0)
    place = lane & 63
    row_place = place[0:1]
    second = lane >= 64
    for t in range(BLOCK):
        real = jnp.where(second, block[:, 64 + t : 65 + t], block[:, t : t + 1])
        imag = jnp.where(second, block[:, 96 + t : 97 + t], block[:, 32 + t : 33 + t])
        row = block[t : t + 1, :]
        swapped = jnp.where(row_place < 32, -turn(row, -32), turn(row, 32))
        inverse = 1.0 / real[t : t + 1, :]
        at_real = row_place == t
        at_imag = row_place == t + 32
        weight = jnp.where(at_real, inverse, jnp.where(at_imag, 0.0, row * inverse))
        crossed = jnp.where(at_real, 0.0, jnp.where(at_imag, inverse, swapped * inverse))
        cleared = jnp.where((place == t) | (place == t + 32), 0.0, block)
        block = jnp.where(sub == t, weight, cleared - real * weight - imag * crossed)
    return block


def invert(z_ref):
    lane = lane_iota((LANES, LANES))
    sub = lax.broadcasted_iota(jnp.int32, (LANES, LANES), 0)
    for k in range(LANES // BLOCK):
        r = k * BLOCK
        p0, q0 = z_ref[0:128, 0:128], z_ref[0:128, 128:256]
        p1, q1 = z_ref[128:256, 0:128], z_ref[128:256, 128:256]
        zero = jnp.zeros_like(p0)
        first = jnp.where(lane < 32, turn(p0, -r), jnp.where(lane < 64, turn(q0, 32 - r), zero))
        second = jnp.where(lane < 64, zero, jnp.where(lane < 96, turn(p1, 64 - r), turn(q1, 96 - r)))
        diagonal = invert_block(first[r : r + 32] + second[r : r + 32])
        small = lane[0:32]
        left = jnp.concatenate(
            [jnp.where(small < 64, diagonal, 0.0), jnp.where(small < 64, 0.0, diagonal)], axis=0
        )

        def stacked(a, b, c, d):
            return jnp.concatenate(
                [
                    jnp.concatenate([a, b], axis=1),
                    jnp.concatenate([-b, a], axis=1),
                    jnp.concatenate([c, d], axis=1),
                    jnp.concatenate([-d, c], axis=1),
                ],
                axis=0,
            )

        rows = slice(r, r + 32)
        w = exact_dot(left, stacked(p0[rows], q0[rows], p1[rows], q1[rows]))
        here = (small >= r) & (small < r + 32)
        wp0 = jnp.where(here, turn(diagonal, r), w[0:32, 0:128])
        wq0 = jnp.where(here, turn(diagonal, r - 32), w[0:32, 128:256])
        wp1 = jnp.where(here, turn(diagonal, r - 64), w[32:64, 0:128])
        wq1 = jnp.where(here, turn(diagonal, r - 96), w[32:64, 128:256])
        inside = (sub >= r) & (sub < r + 32)
        first = jnp.where(inside, jnp.where(sub - r == lane, -1.0, 0.0), first)
        second = jnp.where(inside, jnp.where(sub - r == lane - 64, -1.0, 0.0), second)
        change = exact_dot(jnp.concatenate([first, second], axis=0), stacked(wp0, wq0, wp1, wq1))
        kept = inside | ((lane >= r) & (lane < r + 32))
        for j in range(2):
            for half in range(2):
                tile = (slice(j * 128, j * 128 + 128), slice(half * 128, half * 128 + 128))
                z_ref[tile] = jnp.where(kept, 0.0, z_ref[tile]) - change[tile]


def solve_kernel(ridge_ref, in_ref, out_ref, fields, gram, z):
    for a in range(2):
        for q in range(4):
            for c in range(3):
                for group in range(2):
                    vectors = swap_blocks(
                        in_ref[pl.ds((snap * 16 + group * 8) * 24 + a * 12 + c * 4 + q, 8, stride=24), :]
                        for snap in range(8)
                    )
                    for h in range(8):
                        fields[a, q, pl.ds(((c * 2 + group) * 8 + h) * 8, 8), :] = vectors[h]

    lane = lane_iota((LANES, LANES))
    sub = lax.broadcasted_iota(jnp.int32, (LANES, LANES), 0)
    diagonal = lane == sub
    large = []
    ridges = []
    for j in range(2):
        at = fields[0, 2 * j]
        bt = fields[0, 2 * j + 1]
        real = jnp.transpose(at)
        imag = jnp.transpose(bt)
        left = jnp.concatenate(
            [jnp.concatenate([real, imag], axis=1), jnp.concatenate([imag, -real], axis=1)], axis=0
        )
        both = exact_dot(left, jnp.concatenate([at, bt], axis=0))
        ridge = ridge_ref[j] * float(LANES)
        ridges.append(ridge)
        rows = slice(j * 128, j * 128 + 128)
        gram[rows, 0:128] = both[0:128]
        gram[rows, 128:256] = both[128:256]
        z[rows, 0:128] = both[0:128] + jnp.where(diagonal, ridge, 0.0)
        z[rows, 128:256] = both[128:256]
        trace = jnp.sum(jnp.where(diagonal, both[0:128], 0.0))
        large.append(trace > ridge * float(LANES))
    invert(z)
    misses = jnp.zeros((8, LANES), jnp.float32)
    energy = jnp.zeros((8, LANES), jnp.float32)
    for j in range(2):
        rows = slice(j * 128, j * 128 + 128)
        p, q = gram[rows, 0:128], gram[rows, 128:256]
        ip, iq = z[rows, 0:128], z[rows, 128:256]
        full = jnp.concatenate(
            [jnp.concatenate([p, q], axis=1), jnp.concatenate([-q, p], axis=1)], axis=0
        )
        direct = exact_dot(jnp.concatenate([ip, iq], axis=1), full)
        tp = jnp.where(large[j], jnp.where(diagonal, 1.0, 0.0) - ridges[j] * ip, direct[:, 0:128])
        tq = jnp.where(large[j], -ridges[j] * iq, direct[:, 128:256])
        target = jnp.concatenate([fields[1, 2 * j], fields[1, 2 * j + 1]], axis=1)
        mixing = jnp.concatenate(
            [jnp.concatenate([tp, tq], axis=1), jnp.concatenate([-tq, tp], axis=1)], axis=0
        )
        fitted = exact_dot(target, mixing)
        missed = (target - fitted) ** 2
        square = target**2
        misses += jnp.sum((missed[:, 0:128] + missed[:, 128:256]).reshape(48, 8, LANES), axis=0)
        energy += jnp.sum((square[:, 0:128] + square[:, 128:256]).reshape(48, 8, LANES), axis=0)
        for r in range(2):
            for c in range(3):
                for group in range(2):
                    vectors = swap_blocks(
                        fitted[((c * 2 + group) * 8 + h) * 8 : ((c * 2 + group) * 8 + h) * 8 + 8, r * 128 : r * 128 + 128]
                        for h in range(8)
                    )
                    for snap in range(8):
                        out_ref[
                            pl.ds((snap * 16 + group * 8) * 13 + c * 4 + 2 * j + r, 8, stride=13), :
                        ] = vectors[snap]
    row = lane[0:8]
    sums = jnp.where(row == 0, jnp.sum(misses), jnp.where(row == 1, jnp.sum(energy), 0.0))
    for group in range(16):
        out_ref[pl.ds(group * 8 * 13 + 12, 8, stride=13), :] = sums


def spread_kernel(in_ref, out_ref, misfit_ref):
    for c in range(3):
        for q in range(4):
            tile = jnp.transpose(in_ref[pl.ds(c * 4 + q, LANES, stride=13), :])
            for s in range(16):
                out_ref[pl.ds(s * 96 + c * 32 + q, 8, stride=4), :] = tile[s * 8 : s * 8 + 8]
    sums = jnp.sum(in_ref[pl.ds(12, LANES, stride=13), :], axis=0, keepdims=True)
    lane = lane_iota((1, LANES))
    misses = jnp.sum(jnp.where(lane == 0, sums, 0.0))
    energy = jnp.sum(jnp.where(lane == 1, sums, 0.0))
    misfit_ref[...] = jnp.full((1, LANES), misses, jnp.float32) / jnp.full((1, LANES), energy, jnp.float32)


def vmem():
    return pl.BlockSpec(memory_space=pltpu.VMEM)


def params(**more):
    return pltpu.CompilerParams(vmem_limit_bytes=56 * 1024 * 1024, **more)


def spectra(pairs, table, resolved, drain):
    block = pl.BlockSpec((16, 1, 256, LANES), lambda c: (0, c, 0, 0))
    whole = lambda shape: pl.BlockSpec(shape, lambda c: (0, 0))
    return pl.pallas_call(
        spectrum_kernel,
        grid=(3,),
        in_specs=[whole((2, 256)), whole((256, 256)), block, block],
        out_specs=whole((3072, LANES)),
        out_shape=jax.ShapeDtypeStruct((3072, LANES), jnp.float32),
        scratch_shapes=[
            pltpu.VMEM((512, 4096), jnp.bfloat16),
            pltpu.VMEM((4096, LANES), jnp.float32),
            pltpu.VMEM((256, 4096), jnp.bfloat16),
        ],
        compiler_params=params(dimension_semantics=("arbitrary",)),
    )(pairs, table, resolved, drain)


def settle(ridge, arrived):
    return pl.pallas_call(
        solve_kernel,
        in_specs=[pl.BlockSpec(memory_space=pltpu.SMEM), vmem()],
        out_specs=vmem(),
        out_shape=jax.ShapeDtypeStruct((1664, LANES), jnp.float32),
        scratch_shapes=[
            pltpu.VMEM((2, 4, 384, LANES), jnp.float32),
            pltpu.VMEM((256, 256), jnp.float32),
            pltpu.VMEM((256, 256), jnp.float32),
        ],
        compiler_params=params(),
    )(ridge, arrived)


def spread(returned):
    return pl.pallas_call(
        spread_kernel,
        in_specs=[vmem()],
        out_specs=(vmem(), vmem()),
        out_shape=(
            jax.ShapeDtypeStruct((1536, LANES), jnp.float32),
            jax.ShapeDtypeStruct((1, LANES), jnp.float32),
        ),
        compiler_params=params(),
    )(returned)


def exchange(values, rows):
    moved = lax.all_to_all(
        values.reshape(128, 1, rows * LANES), ("snap", "height"), split_axis=0, concat_axis=0, tiled=True
    )
    return moved.reshape(128 * rows, LANES)


def per_device(resolved, drain, pair_list, ridge_index):
    table = twiddle_rows(resolved.shape[-1])
    sent = spectra(
        pair_list.T,
        table,
        resolved.reshape(16, 3, 256, LANES),
        drain.reshape(16, 3, 256, LANES),
    )
    owner = lax.axis_index("snap") * 16 + lax.axis_index("height")
    levels = lax.dynamic_slice(ridge_index.reshape(2, 128), (0, owner), (2, 1)).reshape(2)
    ridge = 0.25 * jnp.exp2(levels.astype(jnp.float32))
    fitted = settle(ridge, exchange(sent, 24))
    predicted, misfit = spread(exchange(fitted, 13))
    predicted = predicted.reshape(16, 3, 8, 2, 2, 128).transpose(0, 1, 2, 4, 3, 5)
    return (predicted.reshape(16, 3, 8, 2, 256), misfit[0, 0:1])


def solution(mesh):
    return jax.shard_map(
        per_device,
        mesh=mesh,
        in_specs=(
            P("snap", None, "height", None, None, None),
            P("snap", None, "height", None, None, None),
            P(),
            P(),
        ),
        out_specs=(P("snap", None, "height", None, None), P()),
        check_vma=False,
    )
```

time: 791 us -> 104 us (0.13)
  other arithmetic: 400 us -> 0.71 us
  local copies, waits for them, and re-layouts: 211 us -> 1.18 us
  matrix products: 67.3 us -> 0 us
  blocking collectives: 67.2 us -> 22.7 us
  Pallas kernels: 0 us -> 42.5 us
  waiting for transfers between devices: 0.01 us -> 23.9 us
  starting transfers between devices: 32.6 us -> 11.5 us
    another operation x32 -> x0, other arithmetic: 372 us -> none  [the longest x26 245 us: per_device(): factor = jnp.linalg.cholesky(gram)]
    psum x1 -> x0, blocking collectives: 67.2 us -> none  [per_device(): lax.psum((jnp.sum((stacked_y - fitted) ** 2), jnp.sum(stacked_y ** 2)), (...]
    reshape x8 -> x0, local copies, waits for them, and re-layouts: 64.5 us -> none  [the longest x4 40.6 us: spectrum(): product = product.reshape(row_count, mode_count, 2, points)]
    unnamed x46 -> x4, local copies, waits for them, and re-layouts: 50.8 us -> 1.18 us
    pallas_call x0 -> x3, Pallas kernels: none -> 42.5 us  [the longest x1 22.9 us: settle(): pl.pallas_call(solve_kernel, in_specs=[pl.BlockSpec(memory_space=pltpu.SM...]
    another operation x31 -> x0, local copies, waits for them, and re-layouts: 39.9 us -> none
    another operation x32 -> x0, matrix products: 38.1 us -> none  [the longest x10 19.4 us: per_device(): factor = jnp.linalg.cholesky(gram)]
    dot_general x5 -> x0, matrix products: 29.3 us -> none  [the longest x2 11.2 us: spectrum(): jnp.dot(values.reshape(-1, 2 * points), twiddle, preferred_element_type=j...]
  transfers between devices with their start and end apart: 3 -> 1, of which waited for: 0 -> 1; matrix products, arithmetic and copies ran while one was open for 12% -> 1% of each run, Pallas kernels for 0% -> 0%
where the time goes in v1:
time: 104 us; the launch traced here: 103 us
  Pallas kernels  42.5 us (41%)
  waiting for transfers between devices  23.9 us (23%)
  blocking collectives  22.7 us (22%)
  starting transfers between devices  11.5 us (11%)
  local copies, waits for them, and re-layouts  1.18 us (1%)
    all_to_all x1, waiting for transfers between devices, exchange(): lax.all_to_all(values.reshape(128, 1, rows * LANES), ('snap', 'height'),...  23.9 us
    pallas_call x1, Pallas kernels, settle(): pl.pallas_call(solve_kernel, in_specs=[pl.BlockSpec(memory_space=pltpu.SM...  22.9 us
    all_to_all x1, blocking collectives, exchange(): lax.all_to_all(values.reshape(128, 1, rows * LANES), ('snap', 'height'),...  22.7 us
    pallas_call x1, Pallas kernels, spectra(): pl.pallas_call(spectrum_kernel, grid=(3,), in_specs=[whole((2, 256)), who...  17.3 us
    all_to_all x1, starting transfers between devices, exchange(): lax.all_to_all(values.reshape(128, 1, rows * LANES), ('snap', 'height'),...  11.5 us
    pallas_call x1, Pallas kernels, spread(): pl.pallas_call(spread_kernel, in_specs=[vmem()], out_specs=(vmem(), vmem(...  2.35 us
  transfers between devices with their start and end apart: 1, of which 1 were waited for; matrix products, arithmetic and copies ran while one was open for 1% of the time, Pallas kernels for 0%

profile of v1, /device:TPU:1, one launch (start us, length us, event | category | flops | bytes accessed | tf_op | source)
XLA Modules:
  0.0 103.2 jit_solution(897128525817061167)
XLA Ops:
  0.6 17.3 %shard_map.68 = f32[3072,128]{1,0:T(8,128)} custom-call(s32[2,256]{1,0:T(2,128)} %bitcast.21, bf16[256,256]{1,0:T(8,128)(2,1)} %constant.21.clone.table_ref, bf16[16,3,256,128]{3,2,1,0:T(8,128)(2,1)} %bitcast.19, bf16[16,3,256,128]{3,2,1,0:T(8,128)(2,1)} %bitcast.20), custom_call_target="tpu_custom_call" | custom-call | tf_op jit(solution)/shard_map/pallas_call | solution.py:263
  17.9 0.0 copy-start.1
  17.9 11.5 %all-to-all-start = ((f32[128,1,3072]{2,1,0:T(1,128)}), f32[128,1,3072]{2,1,0:T(1,128)S(1)}, u32[]{:S(2)}, u32[]{:S(2)}) async-start(f32[128,1,3072]{2,1,0:T(1,128)} %bitcast.16), calls=%async_computation | async-start | bytes 3145728 | tf_op jit(solution)/shard_map/all_to_all | solution.py:307
  29.4 0.0 copy-done.1
  29.5 0.7 multiply_reduce_fusion.ridge_ref
  30.2 23.9 %all-to-all-done = f32[128,1,3072]{2,1,0:T(1,128)S(1)} async-done(((f32[128,1,3072]{2,1,0:T(1,128)}), f32[128,1,3072]{2,1,0:T(1,128)S(1)}, u32[]{:S(2)}, u32[]{:S(2)}) %all-to-all-start) | async-done | bytes 1572896 | tf_op jit(solution)/shard_map/all_to_all | solution.py:307
  54.1 0.0 copy-start
  54.1 1.2 %copy-done = f32[128,1,3072]{2,1,0:T(1,128)} copy-done((f32[128,1,3072]{2,1,0:T(1,128)}, f32[128,1,3072]{2,1,0:T(1,128)S(1)}, u32[]{:S(2)}) %copy-start) | copy-done | bytes 1572888
  55.3 22.9 %shard_map.69 = f32[1664,128]{1,0:T(8,128)} custom-call(f32[2]{0:T(128)} %multiply_reduce_fusion.ridge_ref, f32[3072,128]{1,0:T(8,128)} %bitcast.15), custom_call_target="tpu_custom_call" | custom-call | tf_op jit(solution)/shard_map/pallas_call | solution.py:279
  78.2 22.7 %all_to_all.10 = f32[128,1,1664]{2,1,0:T(1,128)} all-to-all(f32[128,1,1664]{2,1,0:T(1,128)} %bitcast.18), channel_id=1, replica_groups=mesh['snap'=8,'height'=16] {'snap','height'}, dimensions={0} | all-to-all | bytes 1703936 | tf_op jit(solution)/shard_map/all_to_all | solution.py:307
  100.9 2.3 %shard_map.70 = (f32[1536,128]{1,0:T(8,128)}, f32[1,128]{1,0:T(1,128)}) custom-call(f32[1664,128]{1,0:T(8,128)} %bitcast.17), custom_call_target="tpu_custom_call" | custom-call | tf_op jit(solution)/shard_map/pallas_call | solution.py:294
Async XLA Ops:
  17.9 11.5 %copy-start.1 = (s32[256]{0:T(256)S(1)}, s32[256]{0:T(256)}, u32[]{:S(2)}) copy-start(s32[256]{0:T(256)} %param.8) | copy-start | bytes 3076
  17.9 36.2 %all-to-all-start = ((f32[128,1,3072]{2,1,0:T(1,128)}), f32[128,1,3072]{2,1,0:T(1,128)S(1)}, u32[]{:S(2)}, u32[]{:S(2)}) async-start(f32[128,1,3072]{2,1,0:T(1,128)} %bitcast.16), calls=%async_computation | async-start | bytes 3145728 | tf_op jit(solution)/shard_map/all_to_all | solution.py:307
  54.1 1.2 %copy-start = (f32[128,1,3072]{2,1,0:T(1,128)}, f32[128,1,3072]{2,1,0:T(1,128)S(1)}, u32[]{:S(2)}) copy-start(f32[128,1,3072]{2,1,0:T(1,128)S(1)} %all-to-all-done) | copy-start | bytes 4718596

commit v2 on v1

--- a/solution.py
+++ b/solution.py
@@ -10,7 +10,9 @@
 
 HIGHEST = lax.Precision.HIGHEST
 BLOCK = 32
+GROUP = 8
 LANES = 128
+PITCH = 40
 
 
 def twiddle_rows(length):
@@ -54,7 +56,7 @@
     return values
 
 
-def spectrum_kernel(pairs_ref, table_ref, x_ref, y_ref, out_ref, masked, wide, packed):
+def spectrum_kernel(pairs_ref, table_ref, x_ref, out_ref, masked, wide, packed):
     component = pl.program_id(0)
 
     @pl.when(component == 0)
@@ -77,44 +79,78 @@
                         mode == float(m), rows, 0.0
                     ).astype(jnp.bfloat16)
 
-    for a, ref in enumerate((x_ref, y_ref)):
-        wide[...] = ref[...].reshape(4096, LANES).astype(jnp.float32)
-        for part in range(32):
-            packed[pl.ds(a * LANES, LANES), pl.ds(part * LANES, LANES)] = wide[
-                pl.ds(part, LANES, stride=32), :
-            ].astype(jnp.bfloat16)
+    for group in range(128):
+        first = group % 8 * 32
+        wide[group * PITCH : group * PITCH + 32, :] = x_ref[group // 8, 0, first : first + 32, :].astype(jnp.float32)
+    for part in range(32):
+        packed[:, pl.ds(part * LANES, LANES)] = wide[pl.ds(part, LANES, stride=PITCH), :].astype(jnp.bfloat16)
     product = lax.dot_general(
         masked[...], packed[...], (((1,), (1,)), ((), ())), preferred_element_type=jnp.float32
     )
-    for a in range(2):
-        for q in range(4):
-            for group in range(16):
-                row = q * LANES + group * 8
-                out_ref[pl.ds(group * 8 * 24 + a * 12 + component * 4 + q, 8, stride=24), :] = product[
-                    row : row + 8, a * LANES : (a + 1) * LANES
-                ]
+    for q in range(4):
+        for group in range(16):
+            row = q * LANES + group * 8
+            out_ref[pl.ds(group * 8 * 12 + component * 4 + q, 8, stride=12), :] = product[row : row + 8, :]
+
+
+def spread_row(tiles, t):
+    return jnp.broadcast_to(tiles[t // 8][t % 8 : t % 8 + 1, :], (8, LANES))
 
 
 def invert_block(block):
-    shape = block.shape
-    lane = lane_iota(shape)
-    sub = lax.broadcasted_iota(jnp.int32, shape, 0)
+    count = BLOCK // 8
+    lane = lane_iota((8, LANES))
+    sub = lax.broadcasted_iota(jnp.int32, (8, LANES), 0)
     place = lane & 63
-    row_place = place[0:1]
     second = lane >= 64
-    for t in range(BLOCK):
-        real = jnp.where(second, block[:, 64 + t : 65 + t], block[:, t : t + 1])
-        imag = jnp.where(second, block[:, 96 + t : 97 + t], block[:, 32 + t : 33 + t])
-        row = block[t : t + 1, :]
-        swapped = jnp.where(row_place < 32, -turn(row, -32), turn(row, 32))
-        inverse = 1.0 / real[t : t + 1, :]
-        at_real = row_place == t
-        at_imag = row_place == t + 32
-        weight = jnp.where(at_real, inverse, jnp.where(at_imag, 0.0, row * inverse))
-        crossed = jnp.where(at_real, 0.0, jnp.where(at_imag, inverse, swapped * inverse))
-        cleared = jnp.where((place == t) | (place == t + 32), 0.0, block)
-        block = jnp.where(sub == t, weight, cleared - real * weight - imag * crossed)
-    return block
+    tiles = [block[8 * i : 8 * i + 8] for i in range(count)]
+    turned = [jnp.where(place < 32, -turn(tile, -32), turn(tile, 32)) for tile in tiles]
+    for start in range(0, BLOCK, GROUP):
+        columns = []
+        for t in range(start, start + GROUP):
+            real = [
+                jnp.where(
+                    second,
+                    jnp.broadcast_to(tile[:, 64 + t : 65 + t], (8, LANES)),
+                    jnp.broadcast_to(tile[:, t : t + 1], (8, LANES)),
+                )
+                for tile in tiles
+            ]
+            imag = [
+                jnp.where(
+                    second,
+                    jnp.broadcast_to(tile[:, 96 + t : 97 + t], (8, LANES)),
+                    jnp.broadcast_to(tile[:, 32 + t : 33 + t], (8, LANES)),
+                )
+                for tile in tiles
+            ]
+            columns.append((real, imag))
+        for step in range(GROUP):
+            t = start + step
+            real, imag = columns[step]
+            pivot = sub == t % 8
+            inverse = 1.0 / spread_row(real, t)
+            for later in range(step + 1, GROUP):
+                other_real, other_imag = columns[later]
+                scaled_real = spread_row(other_real, t) * inverse
+                scaled_imag = spread_row(other_imag, t) * inverse
+                new_real = [o - a * scaled_real + b * scaled_imag for o, a, b in zip(other_real, real, imag)]
+                new_imag = [o - a * scaled_imag - b * scaled_real for o, a, b in zip(other_imag, real, imag)]
+                new_real[t // 8] = jnp.where(pivot, scaled_real, new_real[t // 8])
+                new_imag[t // 8] = jnp.where(pivot, scaled_imag, new_imag[t // 8])
+                columns[later] = (new_real, new_imag)
+            row = spread_row(tiles, t)
+            swapped = spread_row(turned, t)
+            at_real = place == t
+            at_imag = place == t + 32
+            weight = jnp.where(at_real, inverse, jnp.where(at_imag, 0.0, row * inverse))
+            crossed = jnp.where(at_real, 0.0, jnp.where(at_imag, inverse, swapped * inverse))
+            gone = at_real | at_imag
+            tiles = [jnp.where(gone, 0.0, o) - a * weight - b * crossed for o, a, b in zip(tiles, real, imag)]
+            tiles[t // 8] = jnp.where(pivot, weight, tiles[t // 8])
+            turned = [jnp.where(gone, 0.0, o) - a * crossed + b * weight for o, a, b in zip(turned, real, imag)]
+            turned[t // 8] = jnp.where(pivot, crossed, turned[t // 8])
+    return jnp.concatenate(tiles, axis=0)
 
 
 def invert(z_ref):
@@ -162,26 +198,28 @@
                 z_ref[tile] = jnp.where(kept, 0.0, z_ref[tile]) - change[tile]
 
 
-def solve_kernel(ridge_ref, in_ref, out_ref, fields, gram, z):
-    for a in range(2):
-        for q in range(4):
-            for c in range(3):
-                for group in range(2):
-                    vectors = swap_blocks(
-                        in_ref[pl.ds((snap * 16 + group * 8) * 24 + a * 12 + c * 4 + q, 8, stride=24), :]
-                        for snap in range(8)
-                    )
-                    for h in range(8):
-                        fields[a, q, pl.ds(((c * 2 + group) * 8 + h) * 8, 8), :] = vectors[h]
-
+def gather_fields(in_ref, fields):
+    for q in range(4):
+        for c in range(3):
+            for group in range(2):
+                vectors = swap_blocks(
+                    in_ref[pl.ds((snap * 16 + group * 8) * 12 + c * 4 + q, 8, stride=12), :]
+                    for snap in range(8)
+                )
+                for h in range(8):
+                    fields[q, pl.ds(((c * 2 + group) * 8 + h) * 8, 8), :] = vectors[h]
+
+
+def operator_kernel(ridge_ref, in_ref, out_ref, fields, gram, z):
+    gather_fields(in_ref, fields)
     lane = lane_iota((LANES, LANES))
     sub = lax.broadcasted_iota(jnp.int32, (LANES, LANES), 0)
     diagonal = lane == sub
     large = []
     ridges = []
     for j in range(2):
-        at = fields[0, 2 * j]
-        bt = fields[0, 2 * j + 1]
+        at = fields[2 * j]
+        bt = fields[2 * j + 1]
         real = jnp.transpose(at)
         imag = jnp.transpose(bt)
         left = jnp.concatenate(
@@ -198,8 +236,6 @@
         trace = jnp.sum(jnp.where(diagonal, both[0:128], 0.0))
         large.append(trace > ridge * float(LANES))
     invert(z)
-    misses = jnp.zeros((8, LANES), jnp.float32)
-    energy = jnp.zeros((8, LANES), jnp.float32)
     for j in range(2):
         rows = slice(j * 128, j * 128 + 128)
         p, q = gram[rows, 0:128], gram[rows, 128:256]
@@ -208,9 +244,20 @@
             [jnp.concatenate([p, q], axis=1), jnp.concatenate([-q, p], axis=1)], axis=0
         )
         direct = exact_dot(jnp.concatenate([ip, iq], axis=1), full)
-        tp = jnp.where(large[j], jnp.where(diagonal, 1.0, 0.0) - ridges[j] * ip, direct[:, 0:128])
-        tq = jnp.where(large[j], -ridges[j] * iq, direct[:, 128:256])
-        target = jnp.concatenate([fields[1, 2 * j], fields[1, 2 * j + 1]], axis=1)
+        out_ref[rows, 0:128] = jnp.where(
+            large[j], jnp.where(diagonal, 1.0, 0.0) - ridges[j] * ip, direct[:, 0:128]
+        )
+        out_ref[rows, 128:256] = jnp.where(large[j], -ridges[j] * iq, direct[:, 128:256])
+
+
+def fit_kernel(operator_ref, in_ref, out_ref, fields):
+    gather_fields(in_ref, fields)
+    misses = jnp.zeros((8, LANES), jnp.float32)
+    energy = jnp.zeros((8, LANES), jnp.float32)
+    for j in range(2):
+        rows = slice(j * 128, j * 128 + 128)
+        tp, tq = operator_ref[rows, 0:128], operator_ref[rows, 128:256]
+        target = jnp.concatenate([fields[2 * j], fields[2 * j + 1]], axis=1)
         mixing = jnp.concatenate(
             [jnp.concatenate([tp, tq], axis=1), jnp.concatenate([-tq, tp], axis=1)], axis=0
         )
@@ -222,15 +269,15 @@
         for r in range(2):
             for c in range(3):
                 for group in range(2):
+                    base = (c * 2 + group) * 64
                     vectors = swap_blocks(
-                        fitted[((c * 2 + group) * 8 + h) * 8 : ((c * 2 + group) * 8 + h) * 8 + 8, r * 128 : r * 128 + 128]
-                        for h in range(8)
+                        fitted[base + h * 8 : base + h * 8 + 8, r * 128 : r * 128 + 128] for h in range(8)
                     )
                     for snap in range(8):
                         out_ref[
                             pl.ds((snap * 16 + group * 8) * 13 + c * 4 + 2 * j + r, 8, stride=13), :
                         ] = vectors[snap]
-    row = lane[0:8]
+    row = lane_iota((8, LANES))
     sums = jnp.where(row == 0, jnp.sum(misses), jnp.where(row == 1, jnp.sum(energy), 0.0))
     for group in range(16):
         out_ref[pl.ds(group * 8 * 13 + 12, 8, stride=13), :] = sums
@@ -257,37 +304,57 @@
     return pltpu.CompilerParams(vmem_limit_bytes=56 * 1024 * 1024, **more)
 
 
-def spectra(pairs, table, resolved, drain):
-    block = pl.BlockSpec((16, 1, 256, LANES), lambda c: (0, c, 0, 0))
+def cost(flops, moved):
+    return pl.CostEstimate(flops=flops, bytes_accessed=moved, transcendentals=0)
+
+
+def spectra(pairs, table, field):
     whole = lambda shape: pl.BlockSpec(shape, lambda c: (0, 0))
     return pl.pallas_call(
         spectrum_kernel,
         grid=(3,),
-        in_specs=[whole((2, 256)), whole((256, 256)), block, block],
-        out_specs=whole((3072, LANES)),
-        out_shape=jax.ShapeDtypeStruct((3072, LANES), jnp.float32),
+        in_specs=[
+            whole((2, 256)),
+            whole((256, 256)),
+            pl.BlockSpec((16, 1, 256, LANES), lambda c: (0, c, 0, 0)),
+        ],
+        out_specs=whole((1536, LANES)),
+        out_shape=jax.ShapeDtypeStruct((1536, LANES), jnp.float32),
         scratch_shapes=[
             pltpu.VMEM((512, 4096), jnp.bfloat16),
-            pltpu.VMEM((4096, LANES), jnp.float32),
-            pltpu.VMEM((256, 4096), jnp.bfloat16),
+            pltpu.VMEM((128 * PITCH, LANES), jnp.float32),
+            pltpu.VMEM((128, 4096), jnp.bfloat16),
         ],
         compiler_params=params(dimension_semantics=("arbitrary",)),
-    )(pairs, table, resolved, drain)
-
-
-def settle(ridge, arrived):
+        cost_estimate=cost(5_000_000_000, 30_000_000),
+    )(pairs, table, field)
+
+
+def operators(ridge, arrived):
     return pl.pallas_call(
-        solve_kernel,
+        operator_kernel,
         in_specs=[pl.BlockSpec(memory_space=pltpu.SMEM), vmem()],
         out_specs=vmem(),
-        out_shape=jax.ShapeDtypeStruct((1664, LANES), jnp.float32),
+        out_shape=jax.ShapeDtypeStruct((256, 256), jnp.float32),
         scratch_shapes=[
-            pltpu.VMEM((2, 4, 384, LANES), jnp.float32),
+            pltpu.VMEM((4, 384, LANES), jnp.float32),
             pltpu.VMEM((256, 256), jnp.float32),
             pltpu.VMEM((256, 256), jnp.float32),
         ],
         compiler_params=params(),
+        cost_estimate=cost(15_000_000_000, 30_000_000),
     )(ridge, arrived)
+
+
+def fit(operator, arrived):
+    return pl.pallas_call(
+        fit_kernel,
+        in_specs=[vmem(), vmem()],
+        out_specs=vmem(),
+        out_shape=jax.ShapeDtypeStruct((1664, LANES), jnp.float32),
+        scratch_shapes=[pltpu.VMEM((4, 384, LANES), jnp.float32)],
+        compiler_params=params(),
+    )(operator, arrived)
 
 
 def spread(returned):
@@ -312,16 +379,14 @@
 
 def per_device(resolved, drain, pair_list, ridge_index):
     table = twiddle_rows(resolved.shape[-1])
-    sent = spectra(
-        pair_list.T,
-        table,
-        resolved.reshape(16, 3, 256, LANES),
-        drain.reshape(16, 3, 256, LANES),
-    )
+    pairs = pair_list.T
+    sent_x = spectra(pairs, table, resolved.reshape(16, 3, 256, LANES))
+    sent_y = spectra(pairs, table, drain.reshape(16, 3, 256, LANES))
     owner = lax.axis_index("snap") * 16 + lax.axis_index("height")
     levels = lax.dynamic_slice(ridge_index.reshape(2, 128), (0, owner), (2, 1)).reshape(2)
     ridge = 0.25 * jnp.exp2(levels.astype(jnp.float32))
-    fitted = settle(ridge, exchange(sent, 24))
+    operator = operators(ridge, exchange(sent_x, 12))
+    fitted = fit(operator, exchange(sent_y, 12))
     predicted, misfit = spread(exchange(fitted, 13))
     predicted = predicted.reshape(16, 3, 8, 2, 2, 128).transpose(0, 1, 2, 4, 3, 5)
     return (predicted.reshape(16, 3, 8, 2, 256), misfit[0, 0:1])

time: 104 us -> 88.3 us (0.85)
  waiting for transfers between devices: 23.9 us -> 13.2 us
  Pallas kernels: 42.5 us -> 33.7 us
  starting transfers between devices: 11.5 us -> 16.1 us
    all_to_all x1 -> x2, waiting for transfers between devices: 23.9 us -> 13.2 us  [exchange(): lax.all_to_all(values.reshape(128, 1, rows * LANES), ('snap', 'height'),...]
    pallas_call x1 -> x2, Pallas kernels: 22.9 us -> 16.9 us  [the longest x1 11.6 us: operators(): pl.pallas_call(operator_kernel, in_specs=[pl.BlockSpec(memory_space=pltpu...]
    all_to_all x1 -> x2, starting transfers between devices: 11.5 us -> 16.1 us  [exchange(): lax.all_to_all(values.reshape(128, 1, rows * LANES), ('snap', 'height'),...]
    pallas_call x1 -> x2, Pallas kernels: 17.3 us -> 14.5 us  [spectra(): pl.pallas_call(spectrum_kernel, grid=(3,), in_specs=[whole((2, 256)), who...]
  transfers between devices with their start and end apart: 1 -> 2, of which waited for: 1 -> 2; matrix products, arithmetic and copies ran while one was open for 1% -> 1% of each run, Pallas kernels for 0% -> 21%
where the time goes in v2:
time: 88.3 us; the launch traced here: 87.9 us
  Pallas kernels  33.7 us (38%)
  blocking collectives  22.6 us (26%)
  starting transfers between devices  16.1 us (18%)
  waiting for transfers between devices  13.2 us (15%)
  local copies, waits for them, and re-layouts  0.89 us (1%)
    all_to_all x1, blocking collectives, exchange(): lax.all_to_all(values.reshape(128, 1, rows * LANES), ('snap', 'height'),...  22.6 us
    all_to_all x2, starting transfers between devices, exchange(): lax.all_to_all(values.reshape(128, 1, rows * LANES), ('snap', 'height'),...  16.1 us
    pallas_call x2, Pallas kernels, spectra(): pl.pallas_call(spectrum_kernel, grid=(3,), in_specs=[whole((2, 256)), who...  14.5 us
    all_to_all x2, waiting for transfers between devices, exchange(): lax.all_to_all(values.reshape(128, 1, rows * LANES), ('snap', 'height'),...  13.2 us
    pallas_call x1, Pallas kernels, operators(): pl.pallas_call(operator_kernel, in_specs=[pl.BlockSpec(memory_space=pltpu...  11.6 us
    pallas_call x1, Pallas kernels, fit(): pl.pallas_call(fit_kernel, in_specs=[vmem(), vmem()], out_specs=vmem(), o...  5.32 us
    pallas_call x1, Pallas kernels, spread(): pl.pallas_call(spread_kernel, in_specs=[vmem()], out_specs=(vmem(), vmem(...  2.35 us
  transfers between devices with their start and end apart: 2, of which 2 were waited for; matrix products, arithmetic and copies ran while one was open for 1% of the time, Pallas kernels for 21%

profile of v2, /device:TPU:1, one launch (start us, length us, event | category | flops | bytes accessed | tf_op | source)
XLA Modules:
  0.0 87.9 jit_solution(6836641550120818420)
XLA Ops:
  0.6 0.0 copy-start.2
  0.6 7.3 %shard_map.68 = f32[1536,128]{1,0:T(8,128)} custom-call(s32[2,256]{1,0:T(2,128)} %bitcast.27, bf16[256,256]{1,0:T(8,128)(2,1)} %constant.21.clone.table_ref, bf16[16,3,256,128]{3,2,1,0:T(8,128)(2,1)} %bitcast.24), custom_call_target="tpu_custom_call" | custom-call | flops 5000000000 | bytes 30000000 | tf_op jit(solution)/shard_map/pallas_call | solution.py:313
  7.9 11.5 %all-to-all-start = ((f32[128,1,1536]{2,1,0:T(1,128)}), f32[128,1,1536]{2,1,0:T(1,128)S(1)}, u32[]{:S(2)}, u32[]{:S(2)}) async-start(f32[128,1,1536]{2,1,0:T(1,128)} %bitcast.21), calls=%async_computation | async-start | bytes 1572864 | tf_op jit(solution)/shard_map/all_to_all | solution.py:374
  19.4 0.0 copy-done.2
  19.4 0.7 multiply_reduce_fusion.ridge_ref
  20.1 7.3 %shard_map.70 = f32[1536,128]{1,0:T(8,128)} custom-call(s32[2,256]{1,0:T(2,128)} %bitcast.28, bf16[256,256]{1,0:T(8,128)(2,1)} %constant.21.clone.table_ref, bf16[16,3,256,128]{3,2,1,0:T(8,128)(2,1)} %bitcast.25), custom_call_target="tpu_custom_call" | custom-call | flops 5000000000 | bytes 30000000 | tf_op jit(solution)/shard_map/pallas_call | solution.py:313
  27.4 8.3 %all-to-all-done = f32[128,1,1536]{2,1,0:T(1,128)S(1)} async-done(((f32[128,1,1536]{2,1,0:T(1,128)}), f32[128,1,1536]{2,1,0:T(1,128)S(1)}, u32[]{:S(2)}, u32[]{:S(2)}) %all-to-all-start) | async-done | bytes 786464 | tf_op jit(solution)/shard_map/all_to_all | solution.py:374
  35.7 0.0 copy-start.1
  35.7 4.6 %all-to-all-start.1 = ((f32[128,1,1536]{2,1,0:T(1,128)}), f32[128,1,1536]{2,1,0:T(1,128)S(1)}, u32[]{:S(2)}, u32[]{:S(2)}) async-start(f32[128,1,1536]{2,1,0:T(1,128)} %bitcast.22), calls=%async_computation.1 | async-start | bytes 1572864 | tf_op jit(solution)/shard_map/all_to_all | solution.py:374
  40.3 0.0 copy-done.1
  40.3 11.6 %shard_map.69.operator_ref = f32[256,256]{1,0:T(8,128)} custom-call(f32[2]{0:T(128)} %multiply_reduce_fusion.ridge_ref, f32[1536,128]{1,0:T(8,128)} %bitcast.20), custom_call_target="tpu_custom_call" | custom-call | flops 15000000512 | bytes 30000000 | tf_op jit(solution)/shard_map/pallas_call | solution.py:334
  51.8 4.9 %all-to-all-done.1 = f32[128,1,1536]{2,1,0:T(1,128)S(1)} async-done(((f32[128,1,1536]{2,1,0:T(1,128)}), f32[128,1,1536]{2,1,0:T(1,128)S(1)}, u32[]{:S(2)}, u32[]{:S(2)}) %all-to-all-start.1) | async-done | bytes 786464 | tf_op jit(solution)/shard_map/all_to_all | solution.py:374
  56.7 0.0 copy-start
  56.7 0.9 copy-done
  57.6 5.3 %shard_map.71 = f32[1664,128]{1,0:T(8,128)} custom-call(f32[256,256]{1,0:T(8,128)} %shard_map.69.operator_ref, f32[1536,128]{1,0:T(8,128)} %bitcast.19), custom_call_target="tpu_custom_call" | custom-call | tf_op jit(solution)/shard_map/pallas_call | solution.py:350
  62.9 22.6 %all_to_all.15 = f32[128,1,1664]{2,1,0:T(1,128)} all-to-all(f32[128,1,1664]{2,1,0:T(1,128)} %bitcast.18), channel_id=1, replica_groups=mesh['snap'=8,'height'=16] {'snap','height'}, dimensions={0} | all-to-all | bytes 1703936 | tf_op jit(solution)/shard_map/all_to_all | solution.py:374
  85.5 2.3 %shard_map.72 = (f32[1536,128]{1,0:T(8,128)}, f32[1,128]{1,0:T(1,128)}) custom-call(f32[1664,128]{1,0:T(8,128)} %bitcast.17), custom_call_target="tpu_custom_call" | custom-call | tf_op jit(solution)/shard_map/pallas_call | solution.py:361
Async XLA Ops:
  0.6 18.8 %copy-start.2 = (s32[256]{0:T(256)S(1)}, s32[256]{0:T(256)}, u32[]{:S(2)}) copy-start(s32[256]{0:T(256)} %param.8) | copy-start | bytes 3076
  7.9 27.8 %all-to-all-start = ((f32[128,1,1536]{2,1,0:T(1,128)}), f32[128,1,1536]{2,1,0:T(1,128)S(1)}, u32[]{:S(2)}, u32[]{:S(2)}) async-start(f32[128,1,1536]{2,1,0:T(1,128)} %bitcast.21), calls=%async_computation | async-start | bytes 1572864 | tf_op jit(solution)/shard_map/all_to_all | solution.py:374
  35.7 4.6 %copy-start.1 = (f32[128,1,1536]{2,1,0:T(1,128)}, f32[128,1,1536]{2,1,0:T(1,128)S(1)}, u32[]{:S(2)}) copy-start(f32[128,1,1536]{2,1,0:T(1,128)S(1)} %all-to-all-done) | copy-start | bytes 2359300
  35.7 21.0 %all-to-all-start.1 = ((f32[128,1,1536]{2,1,0:T(1,128)}), f32[128,1,1536]{2,1,0:T(1,128)S(1)}, u32[]{:S(2)}, u32[]{:S(2)}) async-start(f32[128,1,1536]{2,1,0:T(1,128)} %bitcast.22), calls=%async_computation.1 | async-start | bytes 1572864 | tf_op jit(solution)/shard_map/all_to_all | solution.py:374
  56.7 0.9 %copy-start = (f32[128,1,1536]{2,1,0:T(1,128)}, f32[128,1,1536]{2,1,0:T(1,128)S(1)}, u32[]{:S(2)}) copy-start(f32[128,1,1536]{2,1,0:T(1,128)S(1)} %all-to-all-done.1) | copy-start | bytes 2359300

commit v3 on v1

--- a/solution.py
+++ b/solution.py
@@ -11,6 +11,7 @@
 HIGHEST = lax.Precision.HIGHEST
 BLOCK = 32
 LANES = 128
+PITCH = 33
 
 
 def twiddle_rows(length):
@@ -78,10 +79,14 @@
                     ).astype(jnp.bfloat16)
 
     for a, ref in enumerate((x_ref, y_ref)):
-        wide[...] = ref[...].reshape(4096, LANES).astype(jnp.float32)
+        for group in range(128):
+            first = group % 8 * 32
+            wide[group * PITCH : group * PITCH + 32, :] = ref[group // 8, 0, first : first + 32, :].astype(
+                jnp.float32
+            )
         for part in range(32):
-            packed[pl.ds(a * LANES, LANES), pl.ds(part * LANES, LANES)] = wide[
-                pl.ds(part, LANES, stride=32), :
+            packed[a * LANES : (a + 1) * LANES, pl.ds(part * LANES, LANES)] = wide[
+                pl.ds(part, LANES, stride=PITCH), :
             ].astype(jnp.bfloat16)
     product = lax.dot_general(
         masked[...], packed[...], (((1,), (1,)), ((), ())), preferred_element_type=jnp.float32
@@ -96,25 +101,61 @@
 
 
 def invert_block(block):
-    shape = block.shape
-    lane = lane_iota(shape)
-    sub = lax.broadcasted_iota(jnp.int32, shape, 0)
+    count = BLOCK // 8
+    lane = lane_iota((8, LANES))
+    sub = lax.broadcasted_iota(jnp.int32, (8, LANES), 0)
     place = lane & 63
-    row_place = place[0:1]
     second = lane >= 64
-    for t in range(BLOCK):
-        real = jnp.where(second, block[:, 64 + t : 65 + t], block[:, t : t + 1])
-        imag = jnp.where(second, block[:, 96 + t : 97 + t], block[:, 32 + t : 33 + t])
-        row = block[t : t + 1, :]
-        swapped = jnp.where(row_place < 32, -turn(row, -32), turn(row, 32))
-        inverse = 1.0 / real[t : t + 1, :]
-        at_real = row_place == t
-        at_imag = row_place == t + 32
-        weight = jnp.where(at_real, inverse, jnp.where(at_imag, 0.0, row * inverse))
-        crossed = jnp.where(at_real, 0.0, jnp.where(at_imag, inverse, swapped * inverse))
-        cleared = jnp.where((place == t) | (place == t + 32), 0.0, block)
-        block = jnp.where(sub == t, weight, cleared - real * weight - imag * crossed)
-    return block
+
+    def column(tile, t):
+        def spread_lane(at):
+            return jnp.broadcast_to(tile[:, at : at + 1], (8, LANES))
+
+        return jnp.where(second, spread_lane(64 + t), spread_lane(t))
+
+    def whole_row(tile, t):
+        return jnp.broadcast_to(tile[t : t + 1, :], (8, LANES))
+
+    tiles = [block[8 * i : 8 * i + 8] for i in range(count)]
+    for g in range(count):
+        start = 8 * g
+        tile = tiles[g]
+        turned = jnp.where(place < 32, -turn(tile, -32), turn(tile, 32))
+        columns = [(column(tile, start + t), column(tile, start + t + 32)) for t in range(8)]
+        others = {
+            i: [(column(tiles[i], start + t), column(tiles[i], start + t + 32)) for t in range(8)]
+            for i in range(count)
+            if i != g
+        }
+        for t in range(8):
+            real, imag = columns[t]
+            pivot = sub == t
+            inverse = 1.0 / whole_row(real, t)
+            for later in range(t + 1, 8):
+                other_real, other_imag = columns[later]
+                scaled_real = whole_row(other_real, t) * inverse
+                scaled_imag = whole_row(other_imag, t) * inverse
+                columns[later] = (
+                    jnp.where(pivot, scaled_real, other_real - real * scaled_real + imag * scaled_imag),
+                    jnp.where(pivot, scaled_imag, other_imag - real * scaled_imag - imag * scaled_real),
+                )
+            at_real = place == start + t
+            at_imag = place == start + t + 32
+            gone = at_real | at_imag
+            weight = jnp.where(at_real, inverse, jnp.where(at_imag, 0.0, whole_row(tile, t) * inverse))
+            crossed = jnp.where(at_real, 0.0, jnp.where(at_imag, inverse, whole_row(turned, t) * inverse))
+            tile = jnp.where(pivot, weight, jnp.where(gone, 0.0, tile) - real * weight - imag * crossed)
+            turned = jnp.where(pivot, crossed, jnp.where(gone, 0.0, turned) - real * crossed + imag * weight)
+        tiles[g] = tile
+        within = place & 31
+        gone = (within >= start) & (within < start + 8)
+        rows = [(whole_row(tile, t), whole_row(turned, t)) for t in range(8)]
+        for i, spreads in others.items():
+            changes = [a * weight + b * crossed for (a, b), (weight, crossed) in zip(spreads, rows)]
+            while len(changes) > 1:
+                changes = [u + v for u, v in zip(changes[::2], changes[1::2])]
+            tiles[i] = jnp.where(gone, 0.0, tiles[i]) - changes[0]
+    return jnp.concatenate(tiles, axis=0)
 
 
 def invert(z_ref):
@@ -162,18 +203,21 @@
                 z_ref[tile] = jnp.where(kept, 0.0, z_ref[tile]) - change[tile]
 
 
+def gather_fields(in_ref, fields, a):
+    for q in range(4):
+        for c in range(3):
+            for group in range(2):
+                vectors = swap_blocks(
+                    in_ref[pl.ds((snap * 16 + group * 8) * 24 + a * 12 + c * 4 + q, 8, stride=24), :]
+                    for snap in range(8)
+                )
+                for h in range(8):
+                    fields[a, q, pl.ds(((c * 2 + group) * 8 + h) * 8, 8), :] = vectors[h]
+
+
 def solve_kernel(ridge_ref, in_ref, out_ref, fields, gram, z):
-    for a in range(2):
-        for q in range(4):
-            for c in range(3):
-                for group in range(2):
-                    vectors = swap_blocks(
-                        in_ref[pl.ds((snap * 16 + group * 8) * 24 + a * 12 + c * 4 + q, 8, stride=24), :]
-                        for snap in range(8)
-                    )
-                    for h in range(8):
-                        fields[a, q, pl.ds(((c * 2 + group) * 8 + h) * 8, 8), :] = vectors[h]
-
+    gather_fields(in_ref, fields, 0)
+    owner = lax.axis_index("snap") * 16 + lax.axis_index("height")
     lane = lane_iota((LANES, LANES))
     sub = lax.broadcasted_iota(jnp.int32, (LANES, LANES), 0)
     diagonal = lane == sub
@@ -188,7 +232,7 @@
             [jnp.concatenate([real, imag], axis=1), jnp.concatenate([imag, -real], axis=1)], axis=0
         )
         both = exact_dot(left, jnp.concatenate([at, bt], axis=0))
-        ridge = ridge_ref[j] * float(LANES)
+        ridge = lax.shift_left(jnp.int32(LANES // 4), ridge_ref[j * LANES + owner]).astype(jnp.float32)
         ridges.append(ridge)
         rows = slice(j * 128, j * 128 + 128)
         gram[rows, 0:128] = both[0:128]
@@ -197,6 +241,7 @@
         z[rows, 128:256] = both[128:256]
         trace = jnp.sum(jnp.where(diagonal, both[0:128], 0.0))
         large.append(trace > ridge * float(LANES))
+    gather_fields(in_ref, fields, 1)
     invert(z)
     misses = jnp.zeros((8, LANES), jnp.float32)
     energy = jnp.zeros((8, LANES), jnp.float32)
@@ -222,15 +267,15 @@
         for r in range(2):
             for c in range(3):
                 for group in range(2):
+                    base = (c * 2 + group) * 64
                     vectors = swap_blocks(
-                        fitted[((c * 2 + group) * 8 + h) * 8 : ((c * 2 + group) * 8 + h) * 8 + 8, r * 128 : r * 128 + 128]
-                        for h in range(8)
+                        fitted[base + h * 8 : base + h * 8 + 8, r * 128 : r * 128 + 128] for h in range(8)
                     )
                     for snap in range(8):
                         out_ref[
                             pl.ds((snap * 16 + group * 8) * 13 + c * 4 + 2 * j + r, 8, stride=13), :
                         ] = vectors[snap]
-    row = lane[0:8]
+    row = lane_iota((8, LANES))
     sums = jnp.where(row == 0, jnp.sum(misses), jnp.where(row == 1, jnp.sum(energy), 0.0))
     for group in range(16):
         out_ref[pl.ds(group * 8 * 13 + 12, 8, stride=13), :] = sums
@@ -253,8 +298,8 @@
     return pl.BlockSpec(memory_space=pltpu.VMEM)
 
 
-def params(**more):
-    return pltpu.CompilerParams(vmem_limit_bytes=56 * 1024 * 1024, **more)
+def params(megabytes, **more):
+    return pltpu.CompilerParams(vmem_limit_bytes=megabytes * 1024 * 1024, **more)
 
 
 def spectra(pairs, table, resolved, drain):
@@ -268,14 +313,14 @@
         out_shape=jax.ShapeDtypeStruct((3072, LANES), jnp.float32),
         scratch_shapes=[
             pltpu.VMEM((512, 4096), jnp.bfloat16),
-            pltpu.VMEM((4096, LANES), jnp.float32),
+            pltpu.VMEM((128 * PITCH, LANES), jnp.float32),
             pltpu.VMEM((256, 4096), jnp.bfloat16),
         ],
-        compiler_params=params(dimension_semantics=("arbitrary",)),
+        compiler_params=params(56, dimension_semantics=("arbitrary",)),
     )(pairs, table, resolved, drain)
 
 
-def settle(ridge, arrived):
+def settle(ridge_index, arrived):
     return pl.pallas_call(
         solve_kernel,
         in_specs=[pl.BlockSpec(memory_space=pltpu.SMEM), vmem()],
@@ -286,8 +331,8 @@
             pltpu.VMEM((256, 256), jnp.float32),
             pltpu.VMEM((256, 256), jnp.float32),
         ],
-        compiler_params=params(),
-    )(ridge, arrived)
+        compiler_params=params(24),
+    )(ridge_index, arrived)
 
 
 def spread(returned):
@@ -299,7 +344,7 @@
             jax.ShapeDtypeStruct((1536, LANES), jnp.float32),
             jax.ShapeDtypeStruct((1, LANES), jnp.float32),
         ),
-        compiler_params=params(),
+        compiler_params=params(24),
     )(returned)
 
 
@@ -312,16 +357,11 @@
 
 def per_device(resolved, drain, pair_list, ridge_index):
     table = twiddle_rows(resolved.shape[-1])
+    pairs = pair_list.T
     sent = spectra(
-        pair_list.T,
-        table,
-        resolved.reshape(16, 3, 256, LANES),
-        drain.reshape(16, 3, 256, LANES),
-    )
-    owner = lax.axis_index("snap") * 16 + lax.axis_index("height")
-    levels = lax.dynamic_slice(ridge_index.reshape(2, 128), (0, owner), (2, 1)).reshape(2)
-    ridge = 0.25 * jnp.exp2(levels.astype(jnp.float32))
-    fitted = settle(ridge, exchange(sent, 24))
+        pairs, table, resolved.reshape(16, 3, 256, LANES), drain.reshape(16, 3, 256, LANES)
+    )
+    fitted = settle(ridge_index, exchange(sent, 24))
     predicted, misfit = spread(exchange(fitted, 13))
     predicted = predicted.reshape(16, 3, 8, 2, 2, 128).transpose(0, 1, 2, 4, 3, 5)
     return (predicted.reshape(16, 3, 8, 2, 256), misfit[0, 0:1])

time: 104 us -> 81.5 us (0.78)
  blocking collectives: 22.7 us -> 57.3 us
  waiting for transfers between devices: 23.9 us -> 0 us
  Pallas kernels: 42.5 us -> 23.3 us
  starting transfers between devices: 11.5 us -> 0 us
  local copies, waits for them, and re-layouts: 1.18 us -> 0.01 us
    all_to_all x1 -> x2, blocking collectives: 22.7 us -> 57.3 us  [exchange(): lax.all_to_all(values.reshape(128, 1, rows * LANES), ('snap', 'height'),...]
    all_to_all x1 -> x0, waiting for transfers between devices: 23.9 us -> none  [exchange(): lax.all_to_all(values.reshape(128, 1, rows * LANES), ('snap', 'height'),...]
    all_to_all x1 -> x0, starting transfers between devices: 11.5 us -> none  [exchange(): lax.all_to_all(values.reshape(128, 1, rows * LANES), ('snap', 'height'),...]
    pallas_call x1, Pallas kernels: 22.9 us -> 13 us  [settle(): pl.pallas_call(solve_kernel, in_specs=[pl.BlockSpec(memory_space=pltpu.SM...]
    pallas_call x1, Pallas kernels: 17.3 us -> 9.17 us  [spectra(): pl.pallas_call(spectrum_kernel, grid=(3,), in_specs=[whole((2, 256)), who...]
    unnamed x4 -> x2, local copies, waits for them, and re-layouts: 1.18 us -> 0.01 us
    pallas_call x1, Pallas kernels: 2.35 us -> 1.19 us  [spread(): pl.pallas_call(spread_kernel, in_specs=[vmem()], out_specs=(vmem(), vmem(...]
  transfers between devices with their start and end apart: 1 -> 0, of which waited for: 1 -> 0; matrix products, arithmetic and copies ran while one was open for 1% -> 0% of each run, Pallas kernels for 0% -> 0%
where the time goes in v3:
time: 81.5 us; the launch traced here: 81.3 us
  blocking collectives  57.3 us (70%)
  Pallas kernels  23.3 us (29%)
    all_to_all x2, blocking collectives, exchange(): lax.all_to_all(values.reshape(128, 1, rows * LANES), ('snap', 'height'),...  57.3 us
    pallas_call x1, Pallas kernels, settle(): pl.pallas_call(solve_kernel, in_specs=[pl.BlockSpec(memory_space=pltpu.SM...  13 us
    pallas_call x1, Pallas kernels, spectra(): pl.pallas_call(spectrum_kernel, grid=(3,), in_specs=[whole((2, 256)), who...  9.17 us

profile of v3, /device:TPU:1, one launch (start us, length us, event | category | flops | bytes accessed | tf_op | source)
XLA Modules:
  0.0 81.3 jit_solution(12231436078284150572)
XLA Ops:
  0.6 9.2 %shard_map.68 = f32[3072,128]{1,0:T(8,128)} custom-call(s32[2,256]{1,0:T(2,128)} %bitcast.20, bf16[256,256]{1,0:T(8,128)(2,1)} %constant.2.clone.table_ref, bf16[16,3,256,128]{3,2,1,0:T(8,128)(2,1)} %bitcast.18, bf16[16,3,256,128]{3,2,1,0:T(8,128)(2,1)} %bitcast.19), custom_call_target="tpu_custom_call" | custom-call | tf_op jit(solution)/shard_map/pallas_call | solution.py:308
  9.8 0.0 copy-start
  9.8 36.2 %all_to_all.10 = f32[128,1,3072]{2,1,0:T(1,128)S(1)} all-to-all(f32[128,1,3072]{2,1,0:T(1,128)} %bitcast.17), channel_id=1, replica_groups=mesh['snap'=8,'height'=16] {'snap','height'}, dimensions={0} | all-to-all | bytes 3145728 | tf_op jit(solution)/shard_map/all_to_all | solution.py:352
  46.0 0.0 copy-done
  46.0 13.0 %shard_map.69 = f32[1664,128]{1,0:T(8,128)S(1)} custom-call(s32[256]{0:T(256)S(1)} %copy-done, f32[3072,128]{1,0:T(8,128)S(1)} %bitcast.14), custom_call_target="tpu_custom_call" | custom-call | tf_op jit(solution)/shard_map/pallas_call | solution.py:324
  58.9 21.2 %all_to_all.11 = f32[128,1,1664]{2,1,0:T(1,128)S(1)} all-to-all(f32[128,1,1664]{2,1,0:T(1,128)S(1)} %bitcast.16), channel_id=1, replica_groups=mesh['snap'=8,'height'=16] {'snap','height'}, dimensions={0} | all-to-all | bytes 1703936 | tf_op jit(solution)/shard_map/all_to_all | solution.py:352
  80.1 1.2 %shard_map.70 = (f32[1536,128]{1,0:T(8,128)}, f32[1,128]{1,0:T(1,128)}) custom-call(f32[1664,128]{1,0:T(8,128)S(1)} %bitcast.15), custom_call_target="tpu_custom_call" | custom-call | tf_op jit(solution)/shard_map/pallas_call | solution.py:339
Async XLA Ops:
  9.8 36.2 %copy-start = (s32[256]{0:T(256)S(1)}, s32[256]{0:T(256)}, u32[]{:S(2)}) copy-start(s32[256]{0:T(256)} %ridge_ref.1) | copy-start | bytes 3076

commit v4 on v3

--- a/solution.py
+++ b/solution.py
@@ -228,18 +228,17 @@
         bt = fields[0, 2 * j + 1]
         real = jnp.transpose(at)
         imag = jnp.transpose(bt)
-        left = jnp.concatenate(
-            [jnp.concatenate([real, imag], axis=1), jnp.concatenate([imag, -real], axis=1)], axis=0
-        )
-        both = exact_dot(left, jnp.concatenate([at, bt], axis=0))
+        product = exact_dot(jnp.concatenate([real, imag], axis=0), jnp.concatenate([at, bt], axis=1))
+        p = product[0:128, 0:128] + product[128:256, 128:256]
+        q = product[128:256, 0:128] - product[0:128, 128:256]
         ridge = lax.shift_left(jnp.int32(LANES // 4), ridge_ref[j * LANES + owner]).astype(jnp.float32)
         ridges.append(ridge)
         rows = slice(j * 128, j * 128 + 128)
-        gram[rows, 0:128] = both[0:128]
-        gram[rows, 128:256] = both[128:256]
-        z[rows, 0:128] = both[0:128] + jnp.where(diagonal, ridge, 0.0)
-        z[rows, 128:256] = both[128:256]
-        trace = jnp.sum(jnp.where(diagonal, both[0:128], 0.0))
+        gram[rows, 0:128] = p
+        gram[rows, 128:256] = q
+        z[rows, 0:128] = p + jnp.where(diagonal, ridge, 0.0)
+        z[rows, 128:256] = q
+        trace = jnp.sum(jnp.where(diagonal, p, 0.0))
         large.append(trace > ridge * float(LANES))
     gather_fields(in_ref, fields, 1)
     invert(z)
@@ -247,14 +246,22 @@
     energy = jnp.zeros((8, LANES), jnp.float32)
     for j in range(2):
         rows = slice(j * 128, j * 128 + 128)
-        p, q = gram[rows, 0:128], gram[rows, 128:256]
-        ip, iq = z[rows, 0:128], z[rows, 128:256]
-        full = jnp.concatenate(
-            [jnp.concatenate([p, q], axis=1), jnp.concatenate([-q, p], axis=1)], axis=0
-        )
-        direct = exact_dot(jnp.concatenate([ip, iq], axis=1), full)
-        tp = jnp.where(large[j], jnp.where(diagonal, 1.0, 0.0) - ridges[j] * ip, direct[:, 0:128])
-        tq = jnp.where(large[j], -ridges[j] * iq, direct[:, 128:256])
+        ridge = ridges[j]
+
+        @pl.when(large[j])
+        def _():
+            z[rows, 0:128] = jnp.where(diagonal, 1.0, 0.0) - ridge * z[rows, 0:128]
+            z[rows, 128:256] = -ridge * z[rows, 128:256]
+
+        @pl.when(jnp.logical_not(large[j]))
+        def _():
+            p, q = gram[rows, 0:128], gram[rows, 128:256]
+            full = jnp.concatenate(
+                [jnp.concatenate([p, q], axis=1), jnp.concatenate([-q, p], axis=1)], axis=0
+            )
+            z[rows, :] = exact_dot(z[rows, :], full)
+
+        tp, tq = z[rows, 0:128], z[rows, 128:256]
         target = jnp.concatenate([fields[1, 2 * j], fields[1, 2 * j + 1]], axis=1)
         mixing = jnp.concatenate(
             [jnp.concatenate([tp, tq], axis=1), jnp.concatenate([-tq, tp], axis=1)], axis=0

time: 81.5 us -> 80.3 us (0.985)
  Pallas kernels: 23.3 us -> 22.1 us
    pallas_call x1, Pallas kernels: 13 us -> 11.8 us  [settle(): pl.pallas_call(solve_kernel, in_specs=[pl.BlockSpec(memory_space=pltpu.SM...]
where the time goes in v4:
time: 80.3 us; the launch traced here: 80.1 us
  blocking collectives  57.3 us (71%)
  Pallas kernels  22.1 us (28%)
    all_to_all x2, blocking collectives, exchange(): lax.all_to_all(values.reshape(128, 1, rows * LANES), ('snap', 'height'),...  57.3 us
    pallas_call x1, Pallas kernels, settle(): pl.pallas_call(solve_kernel, in_specs=[pl.BlockSpec(memory_space=pltpu.SM...  11.8 us
    pallas_call x1, Pallas kernels, spectra(): pl.pallas_call(spectrum_kernel, grid=(3,), in_specs=[whole((2, 256)), who...  9.17 us

profile of v4, /device:TPU:1, one launch (start us, length us, event | category | flops | bytes accessed | tf_op | source)
XLA Modules:
  0.0 80.1 jit_solution(7433674869418486127)
XLA Ops:
  0.6 9.2 %shard_map.68 = f32[3072,128]{1,0:T(8,128)} custom-call(s32[2,256]{1,0:T(2,128)} %bitcast.20, bf16[256,256]{1,0:T(8,128)(2,1)} %constant.2.clone.table_ref, bf16[16,3,256,128]{3,2,1,0:T(8,128)(2,1)} %bitcast.18, bf16[16,3,256,128]{3,2,1,0:T(8,128)(2,1)} %bitcast.19), custom_call_target="tpu_custom_call" | custom-call | tf_op jit(solution)/shard_map/pallas_call | solution.py:315
  9.8 0.0 copy-start
  9.8 36.2 %all_to_all.10 = f32[128,1,3072]{2,1,0:T(1,128)S(1)} all-to-all(f32[128,1,3072]{2,1,0:T(1,128)} %bitcast.17), channel_id=1, replica_groups=mesh['snap'=8,'height'=16] {'snap','height'}, dimensions={0} | all-to-all | bytes 3145728 | tf_op jit(solution)/shard_map/all_to_all | solution.py:359
  46.0 0.0 copy-done
  46.0 11.8 %shard_map.69 = f32[1664,128]{1,0:T(8,128)S(1)} custom-call(s32[256]{0:T(256)S(1)} %copy-done, f32[3072,128]{1,0:T(8,128)S(1)} %bitcast.14), custom_call_target="tpu_custom_call" | custom-call | tf_op jit(solution)/shard_map/pallas_call | solution.py:331
  57.8 21.2 %all_to_all.11 = f32[128,1,1664]{2,1,0:T(1,128)S(1)} all-to-all(f32[128,1,1664]{2,1,0:T(1,128)S(1)} %bitcast.16), channel_id=1, replica_groups=mesh['snap'=8,'height'=16] {'snap','height'}, dimensions={0} | all-to-all | bytes 1703936 | tf_op jit(solution)/shard_map/all_to_all | solution.py:359
  78.9 1.2 %shard_map.70 = (f32[1536,128]{1,0:T(8,128)}, f32[1,128]{1,0:T(1,128)}) custom-call(f32[1664,128]{1,0:T(8,128)S(1)} %bitcast.15), custom_call_target="tpu_custom_call" | custom-call | tf_op jit(solution)/shard_map/pallas_call | solution.py:346
Async XLA Ops:
  9.8 36.2 %copy-start = (s32[256]{0:T(256)S(1)}, s32[256]{0:T(256)}, u32[]{:S(2)}) copy-start(s32[256]{0:T(256)} %ridge_ref.1) | copy-start | bytes 3076

commit v5 on v4

--- a/solution.py
+++ b/solution.py
@@ -266,7 +266,13 @@
         mixing = jnp.concatenate(
             [jnp.concatenate([tp, tq], axis=1), jnp.concatenate([-tq, tp], axis=1)], axis=0
         )
-        fitted = exact_dot(target, mixing)
+        fitted = lax.dot_general(
+            target,
+            mixing,
+            (((1,), (0,)), ((), ())),
+            precision=lax.Precision.HIGH,
+            preferred_element_type=jnp.float32,
+        )
         missed = (target - fitted) ** 2
         square = target**2
         misses += jnp.sum((missed[:, 0:128] + missed[:, 128:256]).reshape(48, 8, LANES), axis=0)

time: 80.3 us -> 80 us (level)
  no operation moved by 1% of the time
where the time goes in v5:
time: 80 us; the launch traced here: 79.8 us
  blocking collectives  57.3 us (72%)
  Pallas kernels  21.8 us (27%)
    all_to_all x2, blocking collectives, exchange(): lax.all_to_all(values.reshape(128, 1, rows * LANES), ('snap', 'height'),...  57.3 us
    pallas_call x1, Pallas kernels, settle(): pl.pallas_call(solve_kernel, in_specs=[pl.BlockSpec(memory_space=pltpu.SM...  11.5 us
    pallas_call x1, Pallas kernels, spectra(): pl.pallas_call(spectrum_kernel, grid=(3,), in_specs=[whole((2, 256)), who...  9.17 us

profile of v5, /device:TPU:1, one launch (start us, length us, event | category | flops | bytes accessed | tf_op | source)
XLA Modules:
  0.0 79.8 jit_solution(18305327813941455555)
XLA Ops:
  0.6 9.2 %shard_map.68 = f32[3072,128]{1,0:T(8,128)} custom-call(s32[2,256]{1,0:T(2,128)} %bitcast.20, bf16[256,256]{1,0:T(8,128)(2,1)} %constant.2.clone.table_ref, bf16[16,3,256,128]{3,2,1,0:T(8,128)(2,1)} %bitcast.18, bf16[16,3,256,128]{3,2,1,0:T(8,128)(2,1)} %bitcast.19), custom_call_target="tpu_custom_call" | custom-call | tf_op jit(solution)/shard_map/pallas_call | solution.py:321
  9.8 0.0 copy-start
  9.8 36.2 %all_to_all.10 = f32[128,1,3072]{2,1,0:T(1,128)S(1)} all-to-all(f32[128,1,3072]{2,1,0:T(1,128)} %bitcast.17), channel_id=1, replica_groups=mesh['snap'=8,'height'=16] {'snap','height'}, dimensions={0} | all-to-all | bytes 3145728 | tf_op jit(solution)/shard_map/all_to_all | solution.py:365
  46.0 0.0 copy-done
  46.0 11.5 %shard_map.69 = f32[1664,128]{1,0:T(8,128)S(1)} custom-call(s32[256]{0:T(256)S(1)} %copy-done, f32[3072,128]{1,0:T(8,128)S(1)} %bitcast.14), custom_call_target="tpu_custom_call" | custom-call | tf_op jit(solution)/shard_map/pallas_call | solution.py:337
  57.5 21.1 %all_to_all.11 = f32[128,1,1664]{2,1,0:T(1,128)S(1)} all-to-all(f32[128,1,1664]{2,1,0:T(1,128)S(1)} %bitcast.16), channel_id=1, replica_groups=mesh['snap'=8,'height'=16] {'snap','height'}, dimensions={0} | all-to-all | bytes 1703936 | tf_op jit(solution)/shard_map/all_to_all | solution.py:365
  78.6 1.2 %shard_map.70 = (f32[1536,128]{1,0:T(8,128)}, f32[1,128]{1,0:T(1,128)}) custom-call(f32[1664,128]{1,0:T(8,128)S(1)} %bitcast.15), custom_call_target="tpu_custom_call" | custom-call | tf_op jit(solution)/shard_map/pallas_call | solution.py:352
Async XLA Ops:
  9.8 36.2 %copy-start = (s32[256]{0:T(256)S(1)}, s32[256]{0:T(256)}, u32[]{:S(2)}) copy-start(s32[256]{0:T(256)} %ridge_ref.1) | copy-start | bytes 3076

commit v6 on v4

--- a/solution.py
+++ b/solution.py
@@ -72,10 +72,10 @@
             for r in range(2):
                 rows = jnp.dot(
                     chosen, table_ref[r * LANES : (r + 1) * LANES, :], preferred_element_type=jnp.float32
-                )
+                ).astype(jnp.bfloat16)
                 for m in range(16):
-                    masked[pl.ds((j * 2 + r) * LANES, LANES), pl.ds(m * 256, 256)] = jnp.where(
-                        mode == float(m), rows, 0.0
+                    masked[pl.ds((j * 2 + r) * LANES, LANES), pl.ds(m * 256, 256)] = rows * jnp.where(
+                        mode == float(m), 1.0, 0.0
                     ).astype(jnp.bfloat16)
 
     for a, ref in enumerate((x_ref, y_ref)):

time: 80.3 us -> 80.3 us (level)
  no operation moved by 1% of the time
where the time goes in v6:
time: 80.3 us; the launch traced here: 80.1 us
  blocking collectives  57.3 us (71%)
  Pallas kernels  22.1 us (28%)
    all_to_all x2, blocking collectives, exchange(): lax.all_to_all(values.reshape(128, 1, rows * LANES), ('snap', 'height'),...  57.3 us
    pallas_call x1, Pallas kernels, settle(): pl.pallas_call(solve_kernel, in_specs=[pl.BlockSpec(memory_space=pltpu.SM...  11.8 us
    pallas_call x1, Pallas kernels, spectra(): pl.pallas_call(spectrum_kernel, grid=(3,), in_specs=[whole((2, 256)), who...  9.14 us

profile of v6, /device:TPU:1, one launch (start us, length us, event | category | flops | bytes accessed | tf_op | source)
XLA Modules:
  0.0 80.1 jit_solution(4178722700398974909)
XLA Ops:
  0.6 9.1 %shard_map.68 = f32[3072,128]{1,0:T(8,128)} custom-call(s32[2,256]{1,0:T(2,128)} %bitcast.20, bf16[256,256]{1,0:T(8,128)(2,1)} %constant.2.clone.table_ref, bf16[16,3,256,128]{3,2,1,0:T(8,128)(2,1)} %bitcast.18, bf16[16,3,256,128]{3,2,1,0:T(8,128)(2,1)} %bitcast.19), custom_call_target="tpu_custom_call" | custom-call | tf_op jit(solution)/shard_map/pallas_call | solution.py:315
  9.8 0.0 copy-start
  9.8 36.2 %all_to_all.10 = f32[128,1,3072]{2,1,0:T(1,128)S(1)} all-to-all(f32[128,1,3072]{2,1,0:T(1,128)} %bitcast.17), channel_id=1, replica_groups=mesh['snap'=8,'height'=16] {'snap','height'}, dimensions={0} | all-to-all | bytes 3145728 | tf_op jit(solution)/shard_map/all_to_all | solution.py:359
  45.9 0.0 copy-done
  45.9 11.8 %shard_map.69 = f32[1664,128]{1,0:T(8,128)S(1)} custom-call(s32[256]{0:T(256)S(1)} %copy-done, f32[3072,128]{1,0:T(8,128)S(1)} %bitcast.14), custom_call_target="tpu_custom_call" | custom-call | tf_op jit(solution)/shard_map/pallas_call | solution.py:331
  57.7 21.2 %all_to_all.11 = f32[128,1,1664]{2,1,0:T(1,128)S(1)} all-to-all(f32[128,1,1664]{2,1,0:T(1,128)S(1)} %bitcast.16), channel_id=1, replica_groups=mesh['snap'=8,'height'=16] {'snap','height'}, dimensions={0} | all-to-all | bytes 1703936 | tf_op jit(solution)/shard_map/all_to_all | solution.py:359
  78.9 1.2 %shard_map.70 = (f32[1536,128]{1,0:T(8,128)}, f32[1,128]{1,0:T(1,128)}) custom-call(f32[1664,128]{1,0:T(8,128)S(1)} %bitcast.15), custom_call_target="tpu_custom_call" | custom-call | tf_op jit(solution)/shard_map/pallas_call | solution.py:346
Async XLA Ops:
  9.8 36.2 %copy-start = (s32[256]{0:T(256)S(1)}, s32[256]{0:T(256)}, u32[]{:S(2)}) copy-start(s32[256]{0:T(256)} %ridge_ref.1) | copy-start | bytes 3076
